TPU v7x, 128 devices: a whole 4x4x4 slice. The times are simulated.
128 devices in a mesh: gx: 8 (over y, core), gy: 16 (over x, z).
Axes of the slice: x: 4, y: 4, z: 4, core: 2. Of those that a mesh axis runs over, the one named last changes fastest.
Arguments:
- psi_now: float32 [2, 8, 3072, 3072], P(None, None, 'gy', 'gx'), may hold values from -6 to 6
- potential: float32 [8, 3072, 3072], P(None, 'gy', 'gx'), may hold values from -10 to 0
- surf_cells: int32 [16, 8, 16], P('gy', 'gx'), may hold values from 385 to 73342, as said below
- surf_count: int32 [16, 8], P('gy', 'gx'), may hold values from 0 to 16, as said below
- block_count: int32 [128], replicated, may hold values from 0 to 4, as said below
- block_order: int32 [128], replicated, may hold values from 0 to 127, each once
- amplitude: float32 [512, 128, 2, 128], P(('gx', 'gy')), may hold values from -6 to 6
Outputs:
- psi_next: float32 [2, 8, 3072, 3072], P(None, None, 'gy', 'gx')
- amplitude_next: float32 [512, 128, 2, 128], P(('gx', 'gy'))
Inputs may be any that keep to these rules, and one draw needn't show every extreme that they name: `surf_cells`: A flattened local cell y * 384 + x with 1 <= x <= 382 and 1 <= y <= 190. Live slots hold distinct cells within about half a cell of a circle of radius 1200 cells whose center lies near the middle of the grid; the other slots hold 385. `surf_count`: zero on tiles that the circle misses, at least 1 on the others; 16 on some tiles in every draw. `block_count`: the counts sum to 128; a sixteenth of the groups own 4 planes, an eighth own 2, the others 0 or 1; which groups is drawn.
All inputs are finite; a program needn't handle non-finite values.
Results may differ from a plain program's by a relative error of at most 0.00038.
Values sent between devices are 32-bit elements; how exact they have to be, the bound alone decides.
A program may use at most 256 MiB of HBM per device.

v0:
```python
import functools
import math

import jax
import jax.numpy as jnp
import numpy as np
from jax import lax
from jax.experimental import pallas as pl
from jax.experimental.pallas import tpu as pltpu
from jax.sharding import PartitionSpec as P

spacing = 0.2
kinetic = 12.5
step_dt = 0.016
half_dt = 0.008
start_time = 100.0
later_time = start_time + step_dt
field_peak = 0.05
field_freq = 0.057
k_span = 4.0
flux_weight = 0.0078125
MESH = pl.DeviceIdType.MESH
f32 = jnp.float32


def field_at(moment):
    return field_peak * math.sin(field_freq * moment)


def drift_at(moment):
    return field_peak / (field_freq * field_freq) * math.sin(field_freq * moment)


def mode_weights(planes, modes):
    wave = ((np.arange(modes) - 0.5 * (modes - 1)) * (k_span / modes)).astype(np.float32)
    height = np.float32(spacing) * (np.arange(planes) - 0.5 * (planes - 1)).astype(np.float32)
    out = np.zeros((2, 4 * planes, 4 * modes), np.float32)
    for t, moment in enumerate((start_time, later_time)):
        phase = (
            np.float32(0.5) * wave * wave * np.float32(moment) + wave * np.float32(drift_at(moment))
        )[None, :] - wave[None, :] * height[:, None]
        cos = np.cos(phase.astype(np.float64)).astype(np.float32)
        sin = np.sin(phase.astype(np.float64)).astype(np.float32)
        block = np.block([[cos, sin], [-sin, cos]])
        out[t, : 2 * planes, : 2 * modes] = block
        out[t, 2 * planes :, 2 * modes :] = block
    return out


def iota(shape, dim):
    return lax.broadcasted_iota(jnp.int32, shape, dim)


def step_kernel(
    x_count,
    y_count,
    cells_ref,
    count_ref,
    psi_hbm,
    pot_hbm,
    next_hbm,
    gather_0,
    gather_1,
    live_ref,
    psi_v,
    sec_v,
    pot_v,
    row_msg,
    row_got,
    col_msg,
    col_got,
    corner_got,
    ghost,
    load_sem,
    store_sem,
    row_send,
    row_recv,
    col_send,
    col_recv,
    corner_send,
    corner_recv,
    x_send,
    x_recv,
    y_send,
    y_recv,
):
    gx = lax.axis_index("gx")
    gy = lax.axis_index("gy")
    parts, rows, cols = psi_hbm.shape
    planes = parts // 2
    blocks = rows // 8
    lane_blocks = cols // 128
    top = 8

    def wrap(value, count):
        return lax.rem(value + count, count)

    west, east = wrap(gx - 1, x_count), wrap(gx + 1, x_count)
    north, south = wrap(gy - 1, y_count), wrap(gy + 1, y_count)
    loads = []
    for j in range(lane_blocks):
        sl = slice(128 * j, 128 * j + 128)
        loads.append(
            pltpu.make_async_copy(
                psi_hbm.at[:, :, sl], psi_v.at[j, :, top : top + rows, :], load_sem.at[0, j]
            )
        )
        loads.append(pltpu.make_async_copy(pot_hbm.at[:, :, sl], pot_v.at[j], load_sem.at[1, j]))
    for copy in loads:
        copy.start()

    barrier = pltpu.get_barrier_semaphore()
    for k in range(1, x_count):
        pl.semaphore_signal(barrier, inc=1, device_id=(wrap(gx + k, x_count), gy), device_id_type=MESH)
    for k in range(1, y_count):
        pl.semaphore_signal(barrier, inc=1, device_id=(gx, wrap(gy + k, y_count)), device_id_type=MESH)
    for sx in (west, east):
        for sy in (north, south):
            pl.semaphore_signal(barrier, inc=1, device_id=(sx, sy), device_id_type=MESH)

    for copy in loads:
        copy.wait()

    for side, (near, far) in enumerate(((top, top + 1), (top + rows - 1, top + rows - 2))):
        for j in range(lane_blocks):
            sl = slice(128 * j, 128 * j + 128)
            for p in range(parts):
                row_msg[side, p : p + 1, sl] = psi_v[j, p, near : near + 1, :]
                row_msg[side, parts + p : parts + p + 1, sl] = psi_v[j, p, far : far + 1, :]
            for z in range(planes):
                row_msg[side, 2 * parts + z : 2 * parts + z + 1, sl] = pot_v[
                    j, z, near - top : near - top + 1, :
                ]

    lane8 = iota((8, 128), 1)
    sub8 = iota((8, 128), 0)

    def pack(b, carry):
        r0 = pl.multiple_of(b * 8, 8)
        for side in range(2):
            j = 0 if side == 0 else lane_blocks - 1
            base = 0 if side == 0 else 2
            packed = jnp.zeros((8, 128), f32)
            for p in range(parts):
                block = psi_v[j, p, pl.ds(r0 + top, 8), :]
                packed = jnp.where(lane8 // 2 == p, pltpu.roll(block, (2 * p + base) % 128, 1), packed)
            for z in range(planes):
                block = pot_v[j, z, pl.ds(r0, 8), :]
                packed = jnp.where(
                    lane8 // 2 == 32 + z, pltpu.roll(block, (64 + 2 * z + base) % 128, 1), packed
                )
            col_msg[side, pl.ds(r0, 8), :] = packed
        return carry

    lax.fori_loop(0, blocks, pack, 0)

    pl.semaphore_wait(barrier, x_count - 1 + y_count - 1 + 4)

    halo = []
    for side, target in enumerate((north, south)):
        halo.append(
            pltpu.make_async_remote_copy(
                src_ref=row_msg.at[side],
                dst_ref=row_got.at[1 - side],
                send_sem=row_send.at[side],
                recv_sem=row_recv.at[1 - side],
                device_id=(gx, target),
                device_id_type=MESH,
            )
        )
    for side, target in enumerate((west, east)):
        halo.append(
            pltpu.make_async_remote_copy(
                src_ref=col_msg.at[side],
                dst_ref=col_got.at[1 - side],
                send_sem=col_send.at[side],
                recv_sem=col_recv.at[1 - side],
                device_id=(target, gy),
                device_id_type=MESH,
            )
        )
    for sy, ty in enumerate((north, south)):
        for sx, tx in enumerate((west, east)):
            lo = 0 if sx == 0 else cols - 128
            halo.append(
                pltpu.make_async_remote_copy(
                    src_ref=row_msg.at[sy, 0:parts, lo : lo + 128],
                    dst_ref=corner_got.at[2 * (1 - sy) + 1 - sx],
                    send_sem=corner_send.at[2 * sy + sx],
                    recv_sem=corner_recv.at[2 * (1 - sy) + 1 - sx],
                    device_id=(tx, ty),
                    device_id_type=MESH,
                )
            )
    for copy in halo:
        copy.start()

    lane_p = iota((parts, 128), 1)

    def take(slot, carry):
        out_u, out_d = carry
        cell = cells_ref[slot]
        y = cell // cols
        x = cell - y * cols
        alive = jnp.where(slot < count_ref[0], 1.0, 0.0).astype(f32)
        px = jnp.full((1, 128), spacing * ((gx * cols + x).astype(f32) - (0.5 * cols * x_count - 0.5)), f32)
        py = jnp.full((1, 128), spacing * ((gy * rows + y).astype(f32) - (0.5 * rows * y_count - 0.5)), f32)
        radius = jnp.sqrt(px * px + py * py)
        weight_x = px / radius / (2.0 * spacing) * alive
        weight_y = py / radius / (2.0 * spacing) * alive
        total_u = jnp.zeros((parts, 128), f32)
        total_d = jnp.zeros((parts, 128), f32)
        for j in range(lane_blocks):
            lane = iota((1, 128), 1) + 128 * j
            at = jnp.where(lane == x, alive, 0.0)
            along = jnp.where(lane == x + 1, weight_x, 0.0) - jnp.where(lane == x - 1, weight_x, 0.0)
            across = jnp.where(lane == x, weight_y, 0.0)
            flat = psi_v.at[j].reshape(parts * (rows + 16), 128)
            middle = flat[pl.ds(y + top, parts, stride=rows + 16), :]
            after = flat[pl.ds(y + top + 1, parts, stride=rows + 16), :]
            before = flat[pl.ds(y + top - 1, parts, stride=rows + 16), :]
            total_u = total_u + middle * at
            total_d = total_d + (middle * along + (after - before) * across)
        out_u = jnp.where(lane_p == slot, jnp.sum(total_u, axis=1, keepdims=True), out_u)
        out_d = jnp.where(lane_p == slot, jnp.sum(total_d, axis=1, keepdims=True), out_d)
        return out_u, out_d

    slots = cells_ref.shape[0]

    def surface(target, with_place):
        zero = jnp.zeros((parts, 128), f32)
        out_u, out_d = lax.fori_loop(0, slots, take, (zero, zero), unroll=4)
        turned = jnp.transpose(
            jnp.concatenate([out_u, out_d, jnp.zeros((128 - 2 * parts, 128), f32)], axis=0)
        )
        packed = jnp.where(lane8 < 64, turned[0:8], pltpu.roll(turned[8:16], 64, 1))
        if with_place:
            for slot in range(slots):
                cell = cells_ref[slot]
                y = cell // cols
                x = cell - y * cols
                px = spacing * ((gx * cols + x).astype(f32) - (0.5 * cols * x_count - 0.5))
                py = spacing * ((gy * rows + y).astype(f32) - (0.5 * rows * y_count - 0.5))
                base = 64 * (slot // 8) + 2 * parts
                row = sub8 == slot % 8
                packed = jnp.where(row & (lane8 == base), px, packed)
                packed = jnp.where(row & (lane8 == base + 1), py, packed)
            packed = jnp.where(lane8 == 2 * parts + 2, count_ref[0].astype(f32), packed)
        target[gy, gx] = packed

    def x_copy(buf, phase, k, source):
        return pltpu.make_async_remote_copy(
            src_ref=buf.at[gy, source],
            dst_ref=buf.at[gy, source],
            send_sem=x_send.at[phase, k],
            recv_sem=x_recv.at[phase, k],
            device_id=(wrap(gx + k, x_count), gy),
            device_id_type=MESH,
        )

    def y_copy(buf, phase, k, source):
        return pltpu.make_async_remote_copy(
            src_ref=buf.at[source],
            dst_ref=buf.at[source],
            send_sem=y_send.at[phase, k],
            recv_sem=y_recv.at[phase, k],
            device_id=(gx, wrap(gy + k, y_count)),
            device_id_type=MESH,
        )

    def x_start(buf, phase):
        for k in range(1, x_count):
            x_copy(buf, phase, k, gx).start()

    def x_wait(buf, phase):
        for k in range(1, x_count):
            x_copy(buf, phase, k, wrap(gx - k, x_count)).wait_recv()

    def y_start(buf, phase):
        for k in range(1, y_count):
            y_copy(buf, phase, k, gy).start()

    def y_wait(buf, phase):
        for k in range(1, y_count):
            y_copy(buf, phase, k, wrap(gy - k, y_count)).wait_recv()

    def sends_wait(buf, phase):
        for k in range(1, x_count):
            x_copy(buf, phase, k, gx).wait_send()
        for k in range(1, y_count):
            y_copy(buf, phase, k, gy).wait_send()

    surface(gather_0, True)
    x_start(gather_0, 0)

    for copy in halo:
        copy.wait_recv()

    keep_n = jnp.where(gy > 0, 1.0, 0.0).astype(f32)
    keep_s = jnp.where(gy < y_count - 1, 1.0, 0.0).astype(f32)
    keep_w = jnp.where(gx > 0, 1.0, 0.0).astype(f32)
    keep_e = jnp.where(gx < x_count - 1, 1.0, 0.0).astype(f32)
    field_1 = field_at(start_time)
    field_2 = field_at(later_time)

    def height(index):
        return spacing * (index.astype(f32) - 0.5 * (planes - 1))

    corner_cols = []
    for sy, keep_y in enumerate((keep_n, keep_s)):
        for sx, keep_x in enumerate((keep_w, keep_e)):
            lane = 127 if sx == 0 else 0
            corner_cols.append(corner_got[2 * sy + sx][:, lane : lane + 1] * (keep_y * keep_x))
    lane_row = iota((planes, cols), 1)
    sub_row = iota((planes, cols), 0)
    for side, keep in enumerate((keep_n, keep_s)):
        coeff = step_dt * (
            row_got[side, 2 * parts : 2 * parts + planes, :] + field_1 * height(sub_row) + 6.0 * kinetic
        )
        nears = []
        moves = []
        for part in range(2):
            sl = slice(part * planes, (part + 1) * planes)
            near = row_got[side, sl, :] * keep
            far = row_got[side, parts + part * planes : parts + (part + 1) * planes, :] * keep
            own = row_msg[side, sl, :]
            left = jnp.where(lane_row == 0, corner_cols[2 * side][sl], pltpu.roll(near, 1, 1))
            right = jnp.where(lane_row == cols - 1, corner_cols[2 * side + 1][sl], pltpu.roll(near, cols - 1, 1))
            below = jnp.where(sub_row == 0, 0.0, pltpu.roll(near, 1, 0))
            above = jnp.where(sub_row == planes - 1, 0.0, pltpu.roll(near, planes - 1, 0))
            beside = (far + own) + (left + right) + (below + above)
            nears.append(near)
            moves.append(coeff * near - (step_dt * kinetic) * beside)
        ghost_rows = (nears[0] + moves[1]) * keep, (nears[1] - moves[0]) * keep
        at = top - 1 if side == 0 else top + rows
        for part in range(2):
            for z in range(planes):
                for j in range(lane_blocks):
                    sl = slice(128 * j, 128 * j + 128)
                    psi_v[j, part * planes + z, at : at + 1, :] = nears[part][z : z + 1, sl]
                    sec_v[j, part * planes + z, at : at + 1, :] = ghost_rows[part][z : z + 1, sl]

    lane_c = iota((rows, 128), 1)
    sub_c = iota((rows, 128), 0)
    diag_lane = iota((parts, 128), 1)
    diag_sub = iota((parts, 128), 0)
    plane_c = (lane_c % (2 * planes)) // 2
    for side, keep in enumerate((keep_w, keep_e)):
        got = col_got[side] * keep
        mine = col_msg[side]
        inner = 1 if side == 0 else 127
        odd = 1 if side == 0 else 0
        hit = diag_lane == 2 * diag_sub + odd
        ends = [
            jnp.sum(jnp.where(hit, corner_cols[2 * sy + side], 0.0), axis=0, keepdims=True)
            for sy in range(2)
        ]
        upper = jnp.where(sub_c == 0, ends[0], pltpu.roll(got, 1, 0))
        lower = jnp.where(sub_c == rows - 1, ends[1], pltpu.roll(got, rows - 1, 0))
        below = jnp.where(plane_c == 0, 0.0, pltpu.roll(got, 2, 1))
        above = jnp.where(plane_c == planes - 1, 0.0, pltpu.roll(got, 126, 1))
        beside = (
            (pltpu.roll(got, inner, 1) + pltpu.roll(mine, inner, 1)) + (upper + lower) + (below + above)
        )
        volts = pltpu.roll(got, 64, 1)
        volts = jnp.where(lane_c < 2 * planes, volts, pltpu.roll(volts, 2 * planes, 1))
        coeff = step_dt * (volts + field_1 * height(plane_c) + 6.0 * kinetic)
        move = coeff * got - (step_dt * kinetic) * beside
        ghost[0, side] = got
        ghost[1, side] = (
            got
            + jnp.where(
                lane_c < 2 * planes, pltpu.roll(move, 128 - 2 * planes, 1), -pltpu.roll(move, 2 * planes, 1)
            )
        ) * keep

    first = lane8 == 0
    last = lane8 == 127

    def spread(src, p, r0, stage, b):
        rows_b = pl.ds(r0, 8)
        cur = [src[j, p, rows_b, :] for j in range(lane_blocks)]
        right = [pltpu.roll(c, 1, 1) for c in cur]
        left = [pltpu.roll(c, 127, 1) for c in cur]
        gr = pl.ds(pl.multiple_of(b * 8, 8), 8)
        edge_w = pltpu.roll(ghost[stage, 0, gr, :], (128 - (2 * p + 1)) % 128, 1)
        edge_e = pltpu.roll(ghost[stage, 1, gr, :], (127 - 2 * p) % 128, 1)
        out = []
        for j in range(lane_blocks):
            up = src[j, p, pl.ds(r0 - 1, 8), :]
            down = src[j, p, pl.ds(r0 + 1, 8), :]
            w = jnp.where(first, edge_w if j == 0 else right[j - 1], right[j])
            e = jnp.where(last, edge_e if j == lane_blocks - 1 else left[j + 1], left[j])
            out.append((up + down) + (w + e))
        return cur, out

    def stage_block(src, stage, b, finish):
        r0 = pl.multiple_of(b * 8 + top, 8)
        rows_b = pl.ds(r0, 8)
        dt = step_dt if stage == 0 else half_dt
        field = field_1 if stage == 0 else field_2
        for z in range(planes):
            found = [spread(src, part * planes + z, r0, stage, b) for part in range(2)]
            shift = dt * (field * spacing * (z - 0.5 * (planes - 1)) + 6.0 * kinetic)
            for j in range(lane_blocks):
                coeff = dt * pot_v[j, z, pl.ds(pl.multiple_of(b * 8, 8), 8), :] + shift
                moves = []
                for part in range(2):
                    cur, beside = found[part]
                    p = part * planes + z
                    total = beside[j]
                    if z > 0:
                        total = total + src[j, p - 1, rows_b, :]
                    if z < planes - 1:
                        total = total + src[j, p + 1, rows_b, :]
                    moves.append(coeff * cur[j] - (dt * kinetic) * total)
                finish(z, rows_b, j, found[0][0][j], found[1][0][j], moves)

    def finish_section(z, rows_b, j, real, imag, moves):
        sec_v[j, z, rows_b, :] = real + moves[1]
        sec_v[j, planes + z, rows_b, :] = imag - moves[0]

    def finish_next(z, rows_b, j, real, imag, moves):
        psi_v[j, z, rows_b, :] = 0.5 * (psi_v[j, z, rows_b, :] + real) + moves[1]
        psi_v[j, planes + z, rows_b, :] = 0.5 * (psi_v[j, planes + z, rows_b, :] + imag) - moves[0]

    def run_section(b, carry):
        stage_block(psi_v, 0, b, finish_section)
        return carry

    def run_next(b, carry):
        stage_block(sec_v, 1, b, finish_next)
        return carry

    lax.fori_loop(0, blocks, run_section, 0)
    x_wait(gather_0, 0)
    y_start(gather_0, 0)
    stores = []
    pieces = 4
    per = blocks // pieces
    for q in range(pieces):
        lax.fori_loop(q * per, (q + 1) * per, run_next, 0)
        for j in range(lane_blocks):
            stores.append(
                pltpu.make_async_copy(
                    psi_v.at[j, :, top + 8 * per * q : top + 8 * per * (q + 1), :],
                    next_hbm.at[:, 8 * per * q : 8 * per * (q + 1), 128 * j : 128 * j + 128],
                    store_sem.at[q, j],
                )
            )
            stores[-1].start()
    surface(gather_1, False)
    x_start(gather_1, 1)
    y_wait(gather_0, 0)

    def count_row(i, total):
        for k in range(x_count):
            total = jnp.where(
                lane8 == i * x_count + k, gather_0[i, k][:, 2 * parts + 2 : 2 * parts + 3], total
            )
        return total

    live_ref[...] = lax.fori_loop(0, y_count, count_row, jnp.zeros((8, 128), f32))
    x_wait(gather_1, 1)
    y_start(gather_1, 1)
    for copy in halo:
        copy.wait_send()
    for copy in stores:
        copy.wait()
    y_wait(gather_1, 1)
    sends_wait(gather_0, 0)
    sends_wait(gather_1, 1)


def turns(phase):
    quarter = jnp.floor(phase * 0.6366197723675814 + 0.5)
    rest = phase - quarter * 1.5703125
    rest = rest - quarter * 4.83751296997e-4
    rest = rest - quarter * 7.5497899548918821e-8
    square = rest * rest
    sine = rest + rest * square * (
        -1.6666654611e-1 + square * (8.3321608736e-3 + square * -1.9515295891e-4)
    )
    cosine = (
        1.0
        - 0.5 * square
        + square * square * (4.166664568298827e-2 + square * (-1.388731625493765e-3 + square * 2.443315711809948e-5))
    )
    which = quarter.astype(jnp.int32)
    swap = (which & 1) == 1
    sin_out = jnp.where(swap, cosine, sine)
    cos_out = jnp.where(swap, sine, cosine)
    sin_out = jnp.where((which & 2) == 2, -sin_out, sin_out)
    cos_out = jnp.where(((which + 1) & 2) == 2, -cos_out, cos_out)
    return cos_out, sin_out


def flux_kernel(
    x_count,
    y_count,
    live_ref,
    count_ref,
    order_ref,
    gather_0,
    gather_1,
    weight_ref,
    amp_ref,
    tmp_hbm,
    next_hbm,
    out_ref,
    comp_0,
    comp_1,
    total,
    copy_sem,
):
    copies = []
    parts = tmp_hbm.shape[0]
    quarter = parts // 4
    for q in range(4):
        sl = slice(q * quarter, (q + 1) * quarter)
        copies.append(pltpu.make_async_copy(tmp_hbm.at[sl], next_hbm.at[sl], copy_sem.at[q]))
        copies[-1].start()
    me = lax.axis_index("gx") * y_count + lax.axis_index("gy")
    groups = count_ref.shape[0]
    slots = amp_ref.shape[0]
    features = weight_ref.shape[1]

    def offset(i, at):
        return at + jnp.where(i < me, count_ref[i], 0)

    own_start = lax.fori_loop(0, groups, offset, 0, unroll=8)
    own_count = count_ref[me]
    waves = []
    for s in range(slots):
        plane = order_ref[jnp.minimum(own_start + s, groups - 1)]
        waves.append((plane.astype(f32) - 0.5 * (groups - 1)) * (k_span / groups))

    def gather_tile(t, n):
        c = live_ref[0, t]
        at = pl.ds(pl.multiple_of(t * 8, 8), 8)
        block_0, block_1 = gather_0[at, :], gather_1[at, :]
        to = pl.ds(pl.multiple_of(n * 8, 8), 8)
        comp_0[to, :] = block_0
        comp_1[to, :] = block_1
        n = n + jnp.where(c > 0.5, 1, 0)
        to = pl.ds(pl.multiple_of(n * 8, 8), 8)
        comp_0[to, :] = pltpu.roll(block_0, 64, 1)
        comp_1[to, :] = pltpu.roll(block_1, 64, 1)
        return n + jnp.where(c > 8.5, 1, 0)

    live = lax.fori_loop(0, x_count * y_count, gather_tile, 0, unroll=8)

    def clear(i, carry):
        to = pl.ds(pl.multiple_of((live + i) * 8, 8), 8)
        comp_0[to, :] = jnp.zeros((8, 128), f32)
        comp_1[to, :] = jnp.zeros((8, 128), f32)
        return carry

    lax.fori_loop(0, 16, clear, 0)
    total[...] = jnp.zeros_like(total)
    kx = (iota((128, 128), 0).astype(f32) - 63.5) * (k_span / 128)
    sub8 = iota((8, 128), 0)
    ky = jnp.zeros((8, 128), f32)
    for s in range(slots):
        ky = jnp.where(sub8 // 2 == s, waves[s], ky)
    moment8 = jnp.where(sub8 % 2 == 0, start_time, later_time).astype(f32)

    def chunk(c, carry):
        at = pl.ds(pl.multiple_of(c * 128, 128), 128)
        rows = (comp_0[at, :], comp_1[at, :])
        place = jnp.transpose(rows[0])
        px, py = place[features : features + 1, :], place[features + 1 : features + 2, :]
        col_x, col_y = rows[0][:, features : features + 1], rows[0][:, features + 1 : features + 2]
        square = col_x * col_x + col_y * col_y
        radius = jnp.sqrt(jnp.where(square > 0.0, square, 1.0))
        nx, ny = col_x / radius, col_y / radius
        right = []
        left = []
        for t, moment in enumerate((start_time, later_time)):
            modes = jnp.dot(
                rows[t][:, :features],
                weight_ref[t],
                precision=lax.Precision.HIGHEST,
                preferred_element_type=f32,
            )
            ur, ui, dr, di = (modes[:, 128 * i : 128 * i + 128] for i in range(4))
            right.append(
                jnp.concatenate([nx * ur, ny * ur, dr, nx * ui, ny * ui, di], axis=1).astype(jnp.bfloat16)
            )
            left.append(turns(0.5 * kx * kx * moment - kx * px))
        right = jnp.concatenate(right, axis=0)
        rot_cos, rot_sin = turns(0.5 * ky * ky * moment8 - ky * py)

        for s in range(slots):

            @pl.when(s < own_count)
            def _():
                real = []
                imag = []
                for t in range(2):
                    bc, bs = rot_cos[2 * s + t : 2 * s + t + 1], rot_sin[2 * s + t : 2 * s + t + 1]
                    ac, as_ = left[t]
                    real.append((ac * bc - as_ * bs).astype(jnp.bfloat16))
                    imag.append((ac * bs + as_ * bc).astype(jnp.bfloat16))
                q = jnp.concatenate(
                    [jnp.concatenate(real, axis=1), jnp.concatenate(imag, axis=1)], axis=0
                )
                prod = jnp.dot(q, right, preferred_element_type=f32)
                m = [prod[:128, 128 * i : 128 * i + 128] for i in range(6)]
                w = [prod[128:, 128 * i : 128 * i + 128] for i in range(6)]
                hy = waves[s]
                total[s, 0] += kx * (m[0] - w[3]) + hy * (m[1] - w[4]) + (m[5] + w[2])
                total[s, 1] += kx * (m[3] + w[0]) + hy * (m[4] + w[1]) - (m[2] - w[5])

        return carry

    lax.fori_loop(0, (live + 15) // 16, chunk, 0)
    for s in range(slots):
        for part in range(2):
            sl = pl.ds(part, 128, stride=2)
            inc = jnp.where(s < own_count, (0.5 * flux_weight) * total[s, part], 0.0)
            out_ref[s, sl, :] = amp_ref[s, sl, :] + inc
    for copy in copies:
        copy.wait()


def shards(psi_now, potential, surf_cells, surf_count, block_count, block_order, amplitude):
    x_count = lax.axis_size("gx")
    y_count = lax.axis_size("gy")
    planes, rows, cols = potential.shape
    parts = 2 * planes
    slots = surf_cells.shape[2]
    own, modes_x, _, modes_z = amplitude.shape
    any_spec = pl.BlockSpec(memory_space=pl.ANY)
    vmem = pl.BlockSpec(memory_space=pltpu.VMEM)
    smem = pl.BlockSpec(memory_space=pltpu.SMEM)
    dma = pltpu.SemaphoreType.DMA
    gathered = jax.ShapeDtypeStruct((y_count, x_count, 8, 128), f32)
    field = jax.ShapeDtypeStruct((parts, rows, cols), f32)
    staged, gather_0, gather_1, live = pl.pallas_call(
        functools.partial(step_kernel, x_count, y_count),
        out_shape=(field, gathered, gathered, jax.ShapeDtypeStruct((8, 128), f32)),
        in_specs=[smem, smem, any_spec, any_spec],
        out_specs=(any_spec, vmem, vmem, vmem),
        scratch_shapes=[
            pltpu.VMEM((cols // 128, parts, rows + 16, 128), f32),
            pltpu.VMEM((cols // 128, parts, rows + 16, 128), f32),
            pltpu.VMEM((cols // 128, planes, rows, 128), f32),
            pltpu.VMEM((2, 2 * parts + planes, cols), f32),
            pltpu.VMEM((2, 2 * parts + planes, cols), f32),
            pltpu.VMEM((2, rows, 128), f32),
            pltpu.VMEM((2, rows, 128), f32),
            pltpu.VMEM((4, parts, 128), f32),
            pltpu.VMEM((2, 2, rows, 128), f32),
            dma((2, cols // 128)),
            dma((4, cols // 128)),
            dma((2,)),
            dma((2,)),
            dma((2,)),
            dma((2,)),
            dma((4,)),
            dma((4,)),
            dma((2, x_count)),
            dma((2, x_count)),
            dma((2, y_count)),
            dma((2, y_count)),
        ],
        compiler_params=pltpu.CompilerParams(
            collective_id=0, has_side_effects=True, vmem_limit_bytes=40 * 1024 * 1024
        ),
        name="step",
    )(
        surf_cells.reshape(slots),
        surf_count.reshape(1),
        psi_now.reshape(parts, rows, cols),
        potential,
    )
    tiles = x_count * y_count
    psi_next, amplitude_next = pl.pallas_call(
        functools.partial(flux_kernel, x_count, y_count),
        out_shape=(field, jax.ShapeDtypeStruct((own, 2 * modes_x, modes_z), f32)),
        in_specs=[smem, smem, smem, vmem, vmem, vmem, vmem, any_spec],
        out_specs=(any_spec, vmem),
        scratch_shapes=[
            pltpu.VMEM((slots * tiles + 144, 128), f32),
            pltpu.VMEM((slots * tiles + 144, 128), f32),
            pltpu.VMEM((own, 2, modes_x, modes_z), f32),
            dma((4,)),
        ],
        compiler_params=pltpu.CompilerParams(vmem_limit_bytes=40 * 1024 * 1024),
        name="flux",
    )(
        live,
        block_count,
        block_order,
        gather_0.reshape(tiles * 8, 128),
        gather_1.reshape(tiles * 8, 128),
        jnp.asarray(mode_weights(planes, modes_z)),
        amplitude.reshape(own, 2 * modes_x, modes_z),
        staged,
    )
    return psi_next.reshape(psi_now.shape), amplitude_next.reshape(amplitude.shape)


def solution(mesh):
    return jax.shard_map(
        shards,
        mesh=mesh,
        in_specs=(
            P(None, None, "gy", "gx"),
            P(None, "gy", "gx"),
            P("gy", "gx", None),
            P("gy", "gx"),
            P(),
            P(),
            P(("gx", "gy"), None, None, None),
        ),
        out_specs=(P(None, None, "gy", "gx"), P(("gx", "gy"), None, None, None)),
        check_vma=False,
    )
```

profile of v0, /device:TPU:49, one launch (start us, length us, event | category | flops | bytes accessed | tf_op | source)
XLA Modules:
  0.0 54.1 jit_solution(5022261744219053813)
XLA Ops:
  0.6 0.0 copy-start.5
  0.6 0.0 copy-start.4
  1.3 0.0 copy-start
  1.3 2.3 %copy-done = f32[2,8,192,384]{3,2,1,0:T(8,128)S(1)} copy-done((f32[2,8,192,384]{3,2,1,0:T(8,128)S(1)}, f32[2,8,192,384]{3,2,1,0:T(8,128)}, u32[]{:S(2)}) %copy-start) | copy-done | bytes 4718616
  3.7 0.0 copy-start.1
  3.7 1.7 %copy-done.1 = f32[8,192,384]{2,1,0:T(8,128)S(1)} copy-done((f32[8,192,384]{2,1,0:T(8,128)S(1)}, f32[8,192,384]{2,1,0:T(8,128)}, u32[]{:S(2)}) %copy-start.1) | copy-done | bytes 2359320
  5.3 0.0 copy-start.6
  5.3 0.7 %copy-done.6 = s32[1,1,16]{2,1,0:T(1,128)S(1)} copy-done((s32[1,1,16]{2,1,0:T(1,128)S(1)}, s32[1,1,16]{2,1,0:T(1,128)}, u32[]{:S(2)}) %copy-start.6) | copy-done | bytes 88
  6.0 0.0 copy-start.2
  6.0 0.0 copy-start.3
  6.0 37.4 %step.1 = (f32[16,192,384]{2,1,0:T(8,128)S(1)}, f32[16,8,8,128]{3,2,1,0:T(8,128)S(1)}, f32[16,8,8,128]{3,2,1,0:T(8,128)S(1)}, f32[8,128]{1,0:T(8,128)S(1)}) custom-call(s32[16]{0:T(128)S(1)} %bitcast.13, s32[1]{0:T(128)} %bitcast.8.count_ref, f32[16,192,384]{2,1,0:T(8,128)S(1)} %bitcast.9, f32[8,192,384]{2,1,0:T(8,128)S(1)} %copy-done.1), custom_call_target="tpu_custom_call" | custom-call | tf_op jit(solution)/shard_map/step/pallas_call | solution.py:640
  43.4 0.0 copy-done.5
  43.4 0.0 copy-done.4
  43.4 0.0 copy-done.2
  43.4 0.0 copy-done.3
  43.4 10.6 %flux.1 = (f32[16,192,384]{2,1,0:T(8,128)}, f32[4,256,128]{2,1,0:T(8,128)}) custom-call(f32[8,128]{1,0:T(8,128)S(1)} %get-tuple-element.8.live_ref, s32[128]{0:T(128)S(1)} %copy-done.4, s32[128]{0:T(128)S(1)} %copy-done.5, f32[1024,128]{1,0:T(8,128)S(1)} %bitcast.11, f32[1024,128]{1,0:T(8,128)S(1)} %bitcast.12, f32[2,32,512]{2,1,0:T(8,128)S(1)} %copy-done.3, ...), custom_call_target="tpu_custom_call" | custom-call | tf_op jit(solution)/shard_map/flux/pallas_call | solution.py:679
Async XLA Ops:
  0.6 42.7 %copy-start.5 = (s32[128]{0:T(128)S(1)}, s32[128]{0:T(128)}, u32[]{:S(2)}) copy-start(s32[128]{0:T(128)} %order_ref.1) | copy-start | bytes 1540
  0.6 42.7 %copy-start.4 = (s32[128]{0:T(128)S(1)}, s32[128]{0:T(128)}, u32[]{:S(2)}) copy-start(s32[128]{0:T(128)} %count_ref.1) | copy-start | bytes 1540
  1.3 2.3 %copy-start = (f32[2,8,192,384]{3,2,1,0:T(8,128)S(1)}, f32[2,8,192,384]{3,2,1,0:T(8,128)}, u32[]{:S(2)}) copy-start(f32[2,8,192,384]{3,2,1,0:T(8,128)} %param.8) | copy-start | bytes 14155780
  3.7 1.7 %copy-start.1 = (f32[8,192,384]{2,1,0:T(8,128)S(1)}, f32[8,192,384]{2,1,0:T(8,128)}, u32[]{:S(2)}) copy-start(f32[8,192,384]{2,1,0:T(8,128)} %pot_hbm.1) | copy-start | bytes 7077892
  5.3 0.7 %copy-start.6 = (s32[1,1,16]{2,1,0:T(1,128)S(1)}, s32[1,1,16]{2,1,0:T(1,128)}, u32[]{:S(2)}) copy-start(s32[1,1,16]{2,1,0:T(1,128)} %param.10) | copy-start | bytes 196
  6.0 37.4 %copy-start.2 = (f32[4,128,2,128]{3,2,1,0:T(2,128)S(1)}, f32[4,128,2,128]{3,2,1,0:T(2,128)}, u32[]{:S(2)}) copy-start(f32[4,128,2,128]{3,2,1,0:T(2,128)} %param.14) | copy-start | bytes 1572868
  6.0 37.4 %copy-start.3 = (f32[2,32,512]{2,1,0:T(8,128)S(1)}, f32[2,32,512]{2,1,0:T(8,128)}, u32[]{:S(2)}) copy-start(f32[2,32,512]{2,1,0:T(8,128)} %constant.2.clone.weight_ref) | copy-start | bytes 393220
where the time goes:
time: 54.2 us; the launch traced here: 54.1 us
  Pallas kernels  48 us (89%)
  local copies, waits for them, and re-layouts  4.67 us (9%)
  between operations  1.36 us (3%)
    pallas_call x1, Pallas kernels, shards(): pl.pallas_call(functools.partial(step_kernel, x_count, y_count), out_shap...  37.4 us
    pallas_call x1, Pallas kernels, shards(): pl.pallas_call(functools.partial(flux_kernel, x_count, y_count), out_shap...  10.6 us
    unnamed x14, local copies, waits for them, and re-layouts  4.67 us

commit v1 on v0

--- a/solution.py
+++ b/solution.py
@@ -110,13 +110,23 @@
         copy.start()
 
     barrier = pltpu.get_barrier_semaphore()
-    for k in range(1, x_count):
-        pl.semaphore_signal(barrier, inc=1, device_id=(wrap(gx + k, x_count), gy), device_id_type=MESH)
+    partner = gx + 1 - 2 * lax.rem(gx, 2)
+    column = lax.rem(gx, 2)
+    chip = gx // 2
+    chips = x_count // 2
+    signals = 0
+    for k in range(1, chips):
+        pl.semaphore_signal(
+            barrier, inc=1, device_id=(wrap(gx + 2 * k, x_count), gy), device_id_type=MESH
+        )
+        signals += 1
     for k in range(1, y_count):
         pl.semaphore_signal(barrier, inc=1, device_id=(gx, wrap(gy + k, y_count)), device_id_type=MESH)
+        signals += 1
     for sx in (west, east):
-        for sy in (north, south):
+        for sy in (north, gy, south):
             pl.semaphore_signal(barrier, inc=1, device_id=(sx, sy), device_id_type=MESH)
+            signals += 1
 
     for copy in loads:
         copy.wait()
@@ -152,9 +162,9 @@
             col_msg[side, pl.ds(r0, 8), :] = packed
         return carry
 
-    lax.fori_loop(0, blocks, pack, 0)
-
-    pl.semaphore_wait(barrier, x_count - 1 + y_count - 1 + 4)
+    lax.fori_loop(0, blocks, pack, 0, unroll=2)
+
+    pl.semaphore_wait(barrier, signals)
 
     halo = []
     for side, target in enumerate((north, south)):
@@ -227,14 +237,88 @@
 
     slots = cells_ref.shape[0]
 
-    def surface(target, with_place):
+    half_kin = half_dt * kinetic
+
+    def swap_parts(value):
+        return jnp.concatenate([value[planes:], -value[:planes]], axis=0)
+
+    sub_p = lax.rem(iota((parts, 128), 0), planes)
+    hit_w = lane_p == 2 * iota((parts, 128), 0) + 1
+    hit_e = lane_p == 2 * iota((parts, 128), 0)
+
+    def take_next(slot, carry):
+        out_u, out_d = carry
+        cell = cells_ref[slot]
+        row = cell // cols
+        x = cell - row * cols
+        y = jnp.maximum(row, 1)
+        alive = jnp.where(slot < count_ref[0], 1.0, 0.0).astype(f32)
+        px = jnp.full((1, 128), spacing * ((gx * cols + x).astype(f32) - (0.5 * cols * x_count - 0.5)), f32)
+        py = jnp.full((1, 128), spacing * ((gy * rows + y).astype(f32) - (0.5 * rows * y_count - 0.5)), f32)
+        radius = jnp.sqrt(px * px + py * py)
+        weight_x = px / radius / (2.0 * spacing) * alive
+        weight_y = py / radius / (2.0 * spacing) * alive
+        shift = half_dt * (
+            field_2 * (spacing * (sub_p.astype(f32) - 0.5 * (planes - 1))) + 6.0 * kinetic
+        )
         zero = jnp.zeros((parts, 128), f32)
-        out_u, out_d = lax.fori_loop(0, slots, take, (zero, zero), unroll=4)
+        mean = [zero, zero]
+        plain = [zero, zero]
+        scaled = [zero, zero]
+        around = [zero, zero]
+        for j in range(lane_blocks):
+            lane = iota((1, 128), 1) + 128 * j
+            at = jnp.where(lane == x, alive, 0.0)
+            at_side = jnp.where((lane == x + 1) | (lane == x - 1), alive, 0.0)
+            along = jnp.where(lane == x + 1, weight_x, 0.0) - jnp.where(lane == x - 1, weight_x, 0.0)
+            along_side = jnp.where(lane == x + 2, weight_x, 0.0) - jnp.where(
+                lane == x - 2, weight_x, 0.0
+            )
+            across = jnp.where(lane == x, weight_y, 0.0)
+            across_side = jnp.where((lane == x + 1) | (lane == x - 1), weight_y, 0.0)
+            flat_s = sec_v.at[j].reshape(parts * (rows + 16), 128)
+            flat_f = psi_v.at[j].reshape(parts * (rows + 16), 128)
+            flat_p = pot_v.at[j].reshape(planes * rows, 128)
+            sec = [flat_s[pl.ds(y + top + r, parts, stride=rows + 16), :] for r in range(-2, 3)]
+            psi = [flat_f[pl.ds(y + top + r, parts, stride=rows + 16), :] for r in range(-1, 2)]
+            pot = [flat_p[pl.ds(y + r, planes, stride=rows), :] for r in range(-1, 2)]
+            coeff = [jnp.concatenate([v, v], axis=0) * half_dt + shift for v in pot]
+            mean[0] = mean[0] + (0.5 * at) * (psi[1] + sec[2])
+            plain[0] = plain[0] + at * sec[2]
+            scaled[0] = scaled[0] + at * (coeff[1] * sec[2])
+            around[0] = around[0] + (at * (sec[1] + sec[3]) + at_side * sec[2])
+            mean[1] = mean[1] + 0.5 * (
+                along * (psi[1] + sec[2]) + across * ((psi[2] + sec[3]) - (psi[0] + sec[1]))
+            )
+            plain[1] = plain[1] + (along * sec[2] + across * (sec[3] - sec[1]))
+            scaled[1] = scaled[1] + (
+                along * (coeff[1] * sec[2]) + across * (coeff[2] * sec[3] - coeff[0] * sec[1])
+            )
+            around[1] = around[1] + (
+                (along * (sec[1] + sec[3]) + across * (sec[4] - sec[0]))
+                + (along_side * sec[2] + across_side * (sec[3] - sec[1]))
+            )
+        row_w = ghost[1, 0, pl.ds(y, 1), :] * jnp.where(x == 1, -weight_x, 0.0)
+        row_e = ghost[1, 1, pl.ds(y, 1), :] * jnp.where(x == cols - 2, weight_x, 0.0)
+        around[1] = around[1] + (jnp.where(hit_w, row_w, 0.0) + jnp.where(hit_e, row_e, 0.0))
+        sums = []
+        for i in range(2):
+            below = jnp.where(sub_p == 0, 0.0, pltpu.roll(plain[i], 1, 0))
+            above = jnp.where(sub_p == planes - 1, 0.0, pltpu.roll(plain[i], parts - 1, 0))
+            move = scaled[i] - half_kin * (around[i] + (below + above))
+            sums.append(jnp.sum(mean[i] + swap_parts(move), axis=1, keepdims=True))
+        return jnp.where(lane_p == slot, sums[0], out_u), jnp.where(lane_p == slot, sums[1], out_d)
+
+    def surface(target, is_now):
+        zero = jnp.zeros((parts, 128), f32)
+        out_u, out_d = lax.fori_loop(
+            0, slots, take if is_now else take_next, (zero, zero), unroll=4 if is_now else 2
+        )
         turned = jnp.transpose(
             jnp.concatenate([out_u, out_d, jnp.zeros((128 - 2 * parts, 128), f32)], axis=0)
         )
         packed = jnp.where(lane8 < 64, turned[0:8], pltpu.roll(turned[8:16], 64, 1))
-        if with_place:
+        if is_now:
             for slot in range(slots):
                 cell = cells_ref[slot]
                 y = cell // cols
@@ -246,52 +330,149 @@
                 packed = jnp.where(row & (lane8 == base), px, packed)
                 packed = jnp.where(row & (lane8 == base + 1), py, packed)
             packed = jnp.where(lane8 == 2 * parts + 2, count_ref[0].astype(f32), packed)
-        target[gy, gx] = packed
-
-    def x_copy(buf, phase, k, source):
+        target[column, gy, chip] = packed
+
+    def chip_copy(buf, phase, k, source):
         return pltpu.make_async_remote_copy(
-            src_ref=buf.at[gy, source],
-            dst_ref=buf.at[gy, source],
+            src_ref=buf.at[column, gy, source],
+            dst_ref=buf.at[column, gy, source],
             send_sem=x_send.at[phase, k],
             recv_sem=x_recv.at[phase, k],
-            device_id=(wrap(gx + k, x_count), gy),
+            device_id=(wrap(gx + 2 * k, x_count), gy),
             device_id_type=MESH,
         )
 
     def y_copy(buf, phase, k, source):
         return pltpu.make_async_remote_copy(
-            src_ref=buf.at[source],
-            dst_ref=buf.at[source],
+            src_ref=buf.at[column, source],
+            dst_ref=buf.at[column, source],
             send_sem=y_send.at[phase, k],
             recv_sem=y_recv.at[phase, k],
             device_id=(gx, wrap(gy + k, y_count)),
             device_id_type=MESH,
         )
 
-    def x_start(buf, phase):
-        for k in range(1, x_count):
-            x_copy(buf, phase, k, gx).start()
-
-    def x_wait(buf, phase):
-        for k in range(1, x_count):
-            x_copy(buf, phase, k, wrap(gx - k, x_count)).wait_recv()
-
-    def y_start(buf, phase):
+    def pair_copy(buf, phase, which):
+        return pltpu.make_async_remote_copy(
+            src_ref=buf.at[which],
+            dst_ref=buf.at[which],
+            send_sem=x_send.at[phase, 0],
+            recv_sem=x_recv.at[phase, 0],
+            device_id=(partner, gy),
+            device_id_type=MESH,
+        )
+
+    def hop_1(buf, phase):
+        for k in range(1, chips):
+            chip_copy(buf, phase, k, chip).start()
+
+    def hop_2(buf, phase):
+        for k in range(1, chips):
+            chip_copy(buf, phase, k, wrap(chip - k, chips)).wait_recv()
         for k in range(1, y_count):
             y_copy(buf, phase, k, gy).start()
 
-    def y_wait(buf, phase):
+    def hop_3(buf, phase):
         for k in range(1, y_count):
             y_copy(buf, phase, k, wrap(gy - k, y_count)).wait_recv()
+        pair_copy(buf, phase, column).start()
+
+    def hop_end(buf, phase):
+        pair_copy(buf, phase, 1 - column).wait_recv()
 
     def sends_wait(buf, phase):
-        for k in range(1, x_count):
-            x_copy(buf, phase, k, gx).wait_send()
+        for k in range(1, chips):
+            chip_copy(buf, phase, k, chip).wait_send()
         for k in range(1, y_count):
             y_copy(buf, phase, k, gy).wait_send()
+        pair_copy(buf, phase, column).wait_send()
+
+    field_1 = field_at(start_time)
+    field_2 = field_at(later_time)
+    first = lane8 == 0
+    last = lane8 == 127
+
+    def edges(stage, p, b):
+        at = pl.ds(pl.multiple_of(b * 8, 8), 8)
+        edge_w = pltpu.roll(ghost[stage, 0, at, :], (128 - (2 * p + 1)) % 128, 1)
+        edge_e = pltpu.roll(ghost[stage, 1, at, :], (127 - 2 * p) % 128, 1)
+        return edge_w, edge_e
+
+    def spread(src, p, r0, stage, b):
+        rows_b = pl.ds(r0, 8)
+        cur = [src[j, p, rows_b, :] for j in range(lane_blocks)]
+        right = [pltpu.roll(c, 1, 1) for c in cur]
+        left = [pltpu.roll(c, 127, 1) for c in cur]
+        if stage == 0:
+            edge_w = edge_e = 0.0
+        else:
+            edge_w, edge_e = edges(1, p, b)
+        out = []
+        for j in range(lane_blocks):
+            up = src[j, p, pl.ds(r0 - 1, 8), :]
+            down = src[j, p, pl.ds(r0 + 1, 8), :]
+            w = jnp.where(first, edge_w if j == 0 else right[j - 1], right[j])
+            e = jnp.where(last, edge_e if j == lane_blocks - 1 else left[j + 1], left[j])
+            out.append((up + down) + (w + e))
+        return cur, out
+
+    def stage_block(src, stage, b, finish):
+        r0 = pl.multiple_of(b * 8 + top, 8)
+        rows_b = pl.ds(r0, 8)
+        dt = step_dt if stage == 0 else half_dt
+        field = field_1 if stage == 0 else field_2
+        for z in range(planes):
+            found = [spread(src, part * planes + z, r0, stage, b) for part in range(2)]
+            shift = dt * (field * spacing * (z - 0.5 * (planes - 1)) + 6.0 * kinetic)
+            for j in range(lane_blocks):
+                coeff = dt * pot_v[j, z, pl.ds(pl.multiple_of(b * 8, 8), 8), :] + shift
+                moves = []
+                for part in range(2):
+                    cur, beside = found[part]
+                    p = part * planes + z
+                    total = beside[j]
+                    if z > 0:
+                        total = total + src[j, p - 1, rows_b, :]
+                    if z < planes - 1:
+                        total = total + src[j, p + 1, rows_b, :]
+                    moves.append(coeff * cur[j] - (dt * kinetic) * total)
+                finish(z, rows_b, j, found[0][0][j], found[1][0][j], moves)
+
+    def finish_section(z, rows_b, j, real, imag, moves):
+        sec_v[j, z, rows_b, :] = real + moves[1]
+        sec_v[j, planes + z, rows_b, :] = imag - moves[0]
+
+    def finish_next(z, rows_b, j, real, imag, moves):
+        psi_v[j, z, rows_b, :] = 0.5 * (psi_v[j, z, rows_b, :] + real) + moves[1]
+        psi_v[j, planes + z, rows_b, :] = 0.5 * (psi_v[j, planes + z, rows_b, :] + imag) - moves[0]
+
+    def run_section(b, carry):
+        stage_block(psi_v, 0, b, finish_section)
+        return carry
+
+    def run_next(b, carry):
+        stage_block(sec_v, 1, b, finish_next)
+        return carry
+
+    def fix_columns(b, carry):
+        rows_b = pl.ds(pl.multiple_of(b * 8 + top, 8), 8)
+        for p in range(parts):
+            edge_w, edge_e = edges(0, p, b)
+            other = (p + planes) % parts
+            scale = step_dt * kinetic if p < planes else -step_dt * kinetic
+            sec_v[0, other, rows_b, :] += jnp.where(first, scale * edge_w, 0.0)
+            sec_v[lane_blocks - 1, other, rows_b, :] += jnp.where(last, scale * edge_e, 0.0)
+        return carry
 
     surface(gather_0, True)
-    x_start(gather_0, 0)
+    hop_1(gather_0, 0)
+    clear = jnp.zeros((1, 128), f32)
+    for j in range(lane_blocks):
+        for p in range(parts):
+            psi_v[j, p, top - 1 : top, :] = clear
+            psi_v[j, p, top + rows : top + rows + 1, :] = clear
+    lax.fori_loop(0, blocks, run_section, 0)
+    hop_2(gather_0, 0)
 
     for copy in halo:
         copy.wait_recv()
@@ -300,8 +481,6 @@
     keep_s = jnp.where(gy < y_count - 1, 1.0, 0.0).astype(f32)
     keep_w = jnp.where(gx > 0, 1.0, 0.0).astype(f32)
     keep_e = jnp.where(gx < x_count - 1, 1.0, 0.0).astype(f32)
-    field_1 = field_at(start_time)
-    field_2 = field_at(later_time)
 
     def height(index):
         return spacing * (index.astype(f32) - 0.5 * (planes - 1))
@@ -333,12 +512,16 @@
             moves.append(coeff * near - (step_dt * kinetic) * beside)
         ghost_rows = (nears[0] + moves[1]) * keep, (nears[1] - moves[0]) * keep
         at = top - 1 if side == 0 else top + rows
+        edge = top if side == 0 else top + rows - 1
         for part in range(2):
             for z in range(planes):
                 for j in range(lane_blocks):
                     sl = slice(128 * j, 128 * j + 128)
-                    psi_v[j, part * planes + z, at : at + 1, :] = nears[part][z : z + 1, sl]
-                    sec_v[j, part * planes + z, at : at + 1, :] = ghost_rows[part][z : z + 1, sl]
+                    p = part * planes + z
+                    sec_v[j, p, at : at + 1, :] = ghost_rows[part][z : z + 1, sl]
+                    share = (step_dt * kinetic) * nears[1 - part][z : z + 1, sl]
+                    old = sec_v[j, p, edge : edge + 1, :]
+                    sec_v[j, p, edge : edge + 1, :] = old - share if part == 0 else old + share
 
     lane_c = iota((rows, 128), 1)
     sub_c = iota((rows, 128), 0)
@@ -374,67 +557,9 @@
             )
         ) * keep
 
-    first = lane8 == 0
-    last = lane8 == 127
-
-    def spread(src, p, r0, stage, b):
-        rows_b = pl.ds(r0, 8)
-        cur = [src[j, p, rows_b, :] for j in range(lane_blocks)]
-        right = [pltpu.roll(c, 1, 1) for c in cur]
-        left = [pltpu.roll(c, 127, 1) for c in cur]
-        gr = pl.ds(pl.multiple_of(b * 8, 8), 8)
-        edge_w = pltpu.roll(ghost[stage, 0, gr, :], (128 - (2 * p + 1)) % 128, 1)
-        edge_e = pltpu.roll(ghost[stage, 1, gr, :], (127 - 2 * p) % 128, 1)
-        out = []
-        for j in range(lane_blocks):
-            up = src[j, p, pl.ds(r0 - 1, 8), :]
-            down = src[j, p, pl.ds(r0 + 1, 8), :]
-            w = jnp.where(first, edge_w if j == 0 else right[j - 1], right[j])
-            e = jnp.where(last, edge_e if j == lane_blocks - 1 else left[j + 1], left[j])
-            out.append((up + down) + (w + e))
-        return cur, out
-
-    def stage_block(src, stage, b, finish):
-        r0 = pl.multiple_of(b * 8 + top, 8)
-        rows_b = pl.ds(r0, 8)
-        dt = step_dt if stage == 0 else half_dt
-        field = field_1 if stage == 0 else field_2
-        for z in range(planes):
-            found = [spread(src, part * planes + z, r0, stage, b) for part in range(2)]
-            shift = dt * (field * spacing * (z - 0.5 * (planes - 1)) + 6.0 * kinetic)
-            for j in range(lane_blocks):
-                coeff = dt * pot_v[j, z, pl.ds(pl.multiple_of(b * 8, 8), 8), :] + shift
-                moves = []
-                for part in range(2):
-                    cur, beside = found[part]
-                    p = part * planes + z
-                    total = beside[j]
-                    if z > 0:
-                        total = total + src[j, p - 1, rows_b, :]
-                    if z < planes - 1:
-                        total = total + src[j, p + 1, rows_b, :]
-                    moves.append(coeff * cur[j] - (dt * kinetic) * total)
-                finish(z, rows_b, j, found[0][0][j], found[1][0][j], moves)
-
-    def finish_section(z, rows_b, j, real, imag, moves):
-        sec_v[j, z, rows_b, :] = real + moves[1]
-        sec_v[j, planes + z, rows_b, :] = imag - moves[0]
-
-    def finish_next(z, rows_b, j, real, imag, moves):
-        psi_v[j, z, rows_b, :] = 0.5 * (psi_v[j, z, rows_b, :] + real) + moves[1]
-        psi_v[j, planes + z, rows_b, :] = 0.5 * (psi_v[j, planes + z, rows_b, :] + imag) - moves[0]
-
-    def run_section(b, carry):
-        stage_block(psi_v, 0, b, finish_section)
-        return carry
-
-    def run_next(b, carry):
-        stage_block(sec_v, 1, b, finish_next)
-        return carry
-
-    lax.fori_loop(0, blocks, run_section, 0)
-    x_wait(gather_0, 0)
-    y_start(gather_0, 0)
+    lax.fori_loop(0, blocks, fix_columns, 0, unroll=2)
+    surface(gather_1, False)
+    hop_1(gather_1, 1)
     stores = []
     pieces = 4
     per = blocks // pieces
@@ -449,25 +574,24 @@
                 )
             )
             stores[-1].start()
-    surface(gather_1, False)
-    x_start(gather_1, 1)
-    y_wait(gather_0, 0)
+        if q == 0:
+            hop_2(gather_1, 1)
+            hop_3(gather_0, 0)
+    hop_end(gather_0, 0)
 
     def count_row(i, total):
         for k in range(x_count):
-            total = jnp.where(
-                lane8 == i * x_count + k, gather_0[i, k][:, 2 * parts + 2 : 2 * parts + 3], total
-            )
+            got = gather_0[i // (y_count // 2), lax.rem(i, y_count // 2) * 2 + k // chips, k % chips]
+            total = jnp.where(lane8 == i * x_count + k, got[:, 2 * parts + 2 : 2 * parts + 3], total)
         return total
 
     live_ref[...] = lax.fori_loop(0, y_count, count_row, jnp.zeros((8, 128), f32))
-    x_wait(gather_1, 1)
-    y_start(gather_1, 1)
+    hop_3(gather_1, 1)
     for copy in halo:
         copy.wait_send()
     for copy in stores:
         copy.wait()
-    y_wait(gather_1, 1)
+    hop_end(gather_1, 1)
     sends_wait(gather_0, 0)
     sends_wait(gather_1, 1)
 
@@ -634,13 +758,14 @@
     any_spec = pl.BlockSpec(memory_space=pl.ANY)
     vmem = pl.BlockSpec(memory_space=pltpu.VMEM)
     smem = pl.BlockSpec(memory_space=pltpu.SMEM)
+    hbm = pl.BlockSpec(memory_space=pltpu.HBM)
     dma = pltpu.SemaphoreType.DMA
-    gathered = jax.ShapeDtypeStruct((y_count, x_count, 8, 128), f32)
+    gathered = jax.ShapeDtypeStruct((2, y_count, x_count // 2, 8, 128), f32)
     field = jax.ShapeDtypeStruct((parts, rows, cols), f32)
     staged, gather_0, gather_1, live = pl.pallas_call(
         functools.partial(step_kernel, x_count, y_count),
         out_shape=(field, gathered, gathered, jax.ShapeDtypeStruct((8, 128), f32)),
-        in_specs=[smem, smem, any_spec, any_spec],
+        in_specs=[smem, smem, hbm, hbm],
         out_specs=(any_spec, vmem, vmem, vmem),
         scratch_shapes=[
             pltpu.VMEM((cols // 128, parts, rows + 16, 128), f32),
@@ -666,7 +791,7 @@
             dma((2, y_count)),
         ],
         compiler_params=pltpu.CompilerParams(
-            collective_id=0, has_side_effects=True, vmem_limit_bytes=40 * 1024 * 1024
+            collective_id=0, has_side_effects=True, vmem_limit_bytes=52 * 1024 * 1024
         ),
         name="step",
     )(
@@ -687,7 +812,7 @@
             pltpu.VMEM((own, 2, modes_x, modes_z), f32),
             dma((4,)),
         ],
-        compiler_params=pltpu.CompilerParams(vmem_limit_bytes=40 * 1024 * 1024),
+        compiler_params=pltpu.CompilerParams(vmem_limit_bytes=52 * 1024 * 1024),
         name="flux",
     )(
         live,

time: 54.2 us -> 181 us (3.34)
  the two profiles are of different devices: /device:TPU:49 before, /device:TPU:1 now
where the time goes in v1:
time: 181 us
  Pallas kernels  179 us (99%)
    pallas_call x1, Pallas kernels, shards(): pl.pallas_call(functools.partial(flux_kernel, x_count, y_count), out_shap...  145 us
    pallas_call x1, Pallas kernels, shards(): pl.pallas_call(functools.partial(step_kernel, x_count, y_count), out_shap...  33.7 us

profile of v1, /device:TPU:1, one launch (start us, length us, event | category | flops | bytes accessed | tf_op | source)
XLA Modules:
  0.0 181.2 jit_solution(16911291315267431618)
XLA Ops:
  0.6 0.0 copy-start.1
  0.6 0.0 copy-start
  0.7 0.0 copy-start.3
  0.7 0.0 copy-start.2
  1.4 0.0 copy-start.4
  1.4 0.6 copy-done.4
  2.0 33.7 %step.1 = (f32[16,192,384]{2,1,0:T(8,128)}, f32[2,16,4,8,128]{4,3,2,1,0:T(8,128)S(1)}, f32[2,16,4,8,128]{4,3,2,1,0:T(8,128)S(1)}, f32[8,128]{1,0:T(8,128)S(1)}) custom-call(s32[16]{0:T(128)S(1)} %bitcast.12, s32[1]{0:T(128)} %bitcast.8.count_ref, f32[16,192,384]{2,1,0:T(8,128)} %bitcast.13, f32[8,192,384]{2,1,0:T(8,128)} %pot_hbm.1), custom_call_target="tpu_custom_call" | custom-call | tf_op jit(solution)/shard_map/step/pallas_call | solution.py:765
  35.7 0.0 copy-done.1
  35.7 0.0 copy-done
  35.7 0.0 copy-done.3
  35.8 0.0 copy-done.2
  35.8 145.5 %flux.1 = (f32[16,192,384]{2,1,0:T(8,128)}, f32[4,256,128]{2,1,0:T(8,128)}) custom-call(f32[8,128]{1,0:T(8,128)S(1)} %get-tuple-element.8.live_ref, s32[128]{0:T(128)S(1)} %copy-done.2, s32[128]{0:T(128)S(1)} %copy-done.3, f32[1024,128]{1,0:T(8,128)S(1)} %bitcast.10, f32[1024,128]{1,0:T(8,128)S(1)} %bitcast.11, f32[2,32,512]{2,1,0:T(8,128)S(1)} %copy-done.1, ...), custom_call_target="tpu_custom_call" | custom-call | tf_op jit(solution)/shard_map/flux/pallas_call | solution.py:804
Async XLA Ops:
  0.6 35.1 %copy-start.1 = (f32[2,32,512]{2,1,0:T(8,128)S(1)}, f32[2,32,512]{2,1,0:T(8,128)}, u32[]{:S(2)}) copy-start(f32[2,32,512]{2,1,0:T(8,128)} %constant.2.clone.weight_ref) | copy-start | bytes 393220
  0.6 35.1 %copy-start = (f32[4,128,2,128]{3,2,1,0:T(2,128)S(1)}, f32[4,128,2,128]{3,2,1,0:T(2,128)}, u32[]{:S(2)}) copy-start(f32[4,128,2,128]{3,2,1,0:T(2,128)} %param.14) | copy-start | bytes 1572868
  0.7 35.1 %copy-start.3 = (s32[128]{0:T(128)S(1)}, s32[128]{0:T(128)}, u32[]{:S(2)}) copy-start(s32[128]{0:T(128)} %order_ref.1) | copy-start | bytes 1540
  0.7 35.1 %copy-start.2 = (s32[128]{0:T(128)S(1)}, s32[128]{0:T(128)}, u32[]{:S(2)}) copy-start(s32[128]{0:T(128)} %count_ref.1) | copy-start | bytes 1540
  1.4 0.7 copy-start.4

commit v2 on v1

--- a/solution.py
+++ b/solution.py
@@ -635,6 +635,8 @@
     comp_0,
     comp_1,
     total,
+    held,
+    fetch_sem,
     copy_sem,
 ):
     copies = []
@@ -642,8 +644,9 @@
     quarter = parts // 4
     for q in range(4):
         sl = slice(q * quarter, (q + 1) * quarter)
-        copies.append(pltpu.make_async_copy(tmp_hbm.at[sl], next_hbm.at[sl], copy_sem.at[q]))
-        copies[-1].start()
+        fetch = pltpu.make_async_copy(tmp_hbm.at[sl], held.at[sl], fetch_sem.at[q])
+        fetch.start()
+        copies.append((fetch, pltpu.make_async_copy(held.at[sl], next_hbm.at[sl], copy_sem.at[q])))
     me = lax.axis_index("gx") * y_count + lax.axis_index("gy")
     groups = count_ref.shape[0]
     slots = amp_ref.shape[0]
@@ -681,6 +684,9 @@
         return carry
 
     lax.fori_loop(0, 16, clear, 0)
+    for fetch, copy in copies:
+        fetch.wait()
+        copy.start()
     total[...] = jnp.zeros_like(total)
     kx = (iota((128, 128), 0).astype(f32) - 63.5) * (k_span / 128)
     sub8 = iota((8, 128), 0)
@@ -744,7 +750,7 @@
             sl = pl.ds(part, 128, stride=2)
             inc = jnp.where(s < own_count, (0.5 * flux_weight) * total[s, part], 0.0)
             out_ref[s, sl, :] = amp_ref[s, sl, :] + inc
-    for copy in copies:
+    for fetch, copy in copies:
         copy.wait()
 
 
@@ -810,6 +816,8 @@
             pltpu.VMEM((slots * tiles + 144, 128), f32),
             pltpu.VMEM((slots * tiles + 144, 128), f32),
             pltpu.VMEM((own, 2, modes_x, modes_z), f32),
+            pltpu.VMEM((parts, rows, cols), f32),
+            dma((4,)),
             dma((4,)),
         ],
         compiler_params=pltpu.CompilerParams(vmem_limit_bytes=52 * 1024 * 1024),

time: 181 us -> 44.9 us (0.25)
  the two profiles are of different devices: /device:TPU:1 before, /device:TPU:32 now
where the time goes in v2:
time: 44.9 us; the launch traced here: 44.7 us
  Pallas kernels  42.7 us (95%)
  between operations  1.42 us (3%)
  local copies, waits for them, and re-layouts  0.67 us (1%)
    pallas_call x1, Pallas kernels, shards(): pl.pallas_call(functools.partial(step_kernel, x_count, y_count), out_shap...  31.4 us
    pallas_call x1, Pallas kernels, shards(): pl.pallas_call(functools.partial(flux_kernel, x_count, y_count), out_shap...  11.3 us

profile of v2, /device:TPU:32, one launch (start us, length us, event | category | flops | bytes accessed | tf_op | source)
XLA Modules:
  0.0 44.7 jit_solution(17077804588207575639)
XLA Ops:
  0.6 0.0 copy-start.1
  0.6 0.0 copy-start
  0.7 0.0 copy-start.3
  0.7 0.0 copy-start.2
  1.4 0.0 copy-start.4
  1.4 0.6 %copy-done.4 = s32[1,1,16]{2,1,0:T(1,128)S(1)} copy-done((s32[1,1,16]{2,1,0:T(1,128)S(1)}, s32[1,1,16]{2,1,0:T(1,128)}, u32[]{:S(2)}) %copy-start.4) | copy-done | bytes 88
  2.0 31.4 %step.1 = (f32[16,192,384]{2,1,0:T(8,128)}, f32[2,16,4,8,128]{4,3,2,1,0:T(8,128)S(1)}, f32[2,16,4,8,128]{4,3,2,1,0:T(8,128)S(1)}, f32[8,128]{1,0:T(8,128)S(1)}) custom-call(s32[16]{0:T(128)S(1)} %bitcast.12, s32[1]{0:T(128)} %bitcast.8.count_ref, f32[16,192,384]{2,1,0:T(8,128)} %bitcast.13, f32[8,192,384]{2,1,0:T(8,128)} %pot_hbm.1), custom_call_target="tpu_custom_call" | custom-call | tf_op jit(solution)/shard_map/step/pallas_call | solution.py:771
  33.4 0.0 copy-done.1
  33.4 0.0 copy-done
  33.4 0.0 copy-done.3
  33.4 0.0 copy-done.2
  33.4 11.3 %flux.1 = (f32[16,192,384]{2,1,0:T(8,128)}, f32[4,256,128]{2,1,0:T(8,128)}) custom-call(f32[8,128]{1,0:T(8,128)S(1)} %get-tuple-element.8.live_ref, s32[128]{0:T(128)S(1)} %copy-done.2, s32[128]{0:T(128)S(1)} %copy-done.3, f32[1024,128]{1,0:T(8,128)S(1)} %bitcast.10, f32[1024,128]{1,0:T(8,128)S(1)} %bitcast.11, f32[2,32,512]{2,1,0:T(8,128)S(1)} %copy-done.1, ...), custom_call_target="tpu_custom_call" | custom-call | tf_op jit(solution)/shard_map/flux/pallas_call | solution.py:810
Async XLA Ops:
  0.6 32.8 %copy-start.1 = (f32[2,32,512]{2,1,0:T(8,128)S(1)}, f32[2,32,512]{2,1,0:T(8,128)}, u32[]{:S(2)}) copy-start(f32[2,32,512]{2,1,0:T(8,128)} %constant.2.clone.weight_ref) | copy-start | bytes 393220
  0.6 32.8 %copy-start = (f32[4,128,2,128]{3,2,1,0:T(2,128)S(1)}, f32[4,128,2,128]{3,2,1,0:T(2,128)}, u32[]{:S(2)}) copy-start(f32[4,128,2,128]{3,2,1,0:T(2,128)} %param.14) | copy-start | bytes 1572868
  0.7 32.8 %copy-start.3 = (s32[128]{0:T(128)S(1)}, s32[128]{0:T(128)}, u32[]{:S(2)}) copy-start(s32[128]{0:T(128)} %order_ref.1) | copy-start | bytes 1540
  0.7 32.8 %copy-start.2 = (s32[128]{0:T(128)S(1)}, s32[128]{0:T(128)}, u32[]{:S(2)}) copy-start(s32[128]{0:T(128)} %count_ref.1) | copy-start | bytes 1540
  1.4 0.7 %copy-start.4 = (s32[1,1,16]{2,1,0:T(1,128)S(1)}, s32[1,1,16]{2,1,0:T(1,128)}, u32[]{:S(2)}) copy-start(s32[1,1,16]{2,1,0:T(1,128)} %param.10) | copy-start | bytes 196

commit v3 on v2

--- a/solution.py
+++ b/solution.py
@@ -44,7 +44,11 @@
         block = np.block([[cos, sin], [-sin, cos]])
         out[t, : 2 * planes, : 2 * modes] = block
         out[t, 2 * planes :, 2 * modes :] = block
-    return out
+    high = out.astype(jnp.bfloat16).astype(np.float32)
+    mid = (out - high).astype(jnp.bfloat16).astype(np.float32)
+    low = out - high - mid
+    none = np.zeros_like(out)
+    return np.concatenate([high, high, high, mid, low, mid, none, none], axis=1).astype(jnp.bfloat16)
 
 
 def iota(shape, dim):
@@ -150,19 +154,26 @@
         for side in range(2):
             j = 0 if side == 0 else lane_blocks - 1
             base = 0 if side == 0 else 2
-            packed = jnp.zeros((8, 128), f32)
-            for p in range(parts):
-                block = psi_v[j, p, pl.ds(r0 + top, 8), :]
-                packed = jnp.where(lane8 // 2 == p, pltpu.roll(block, (2 * p + base) % 128, 1), packed)
-            for z in range(planes):
-                block = pot_v[j, z, pl.ds(r0, 8), :]
-                packed = jnp.where(
-                    lane8 // 2 == 32 + z, pltpu.roll(block, (64 + 2 * z + base) % 128, 1), packed
-                )
+            moved = [
+                (p, pltpu.roll(psi_v[j, p, pl.ds(r0 + top, 8), :], (2 * p + base) % 128, 1))
+                for p in range(parts)
+            ] + [
+                (32 + z, pltpu.roll(pot_v[j, z, pl.ds(r0, 8), :], (64 + 2 * z + base) % 128, 1))
+                for z in range(planes)
+            ]
+            while len(moved) > 1:
+                joined = []
+                for i in range(0, len(moved) - 1, 2):
+                    (at_a, part_a), (at_b, part_b) = moved[i], moved[i + 1]
+                    joined.append((at_a, jnp.where(lane8 < 2 * at_b, part_a, part_b)))
+                if len(moved) % 2:
+                    joined.append(moved[-1])
+                moved = joined
+            packed = moved[0][1]
             col_msg[side, pl.ds(r0, 8), :] = packed
         return carry
 
-    lax.fori_loop(0, blocks, pack, 0, unroll=2)
+    lax.fori_loop(0, blocks, pack, 0, unroll=4)
 
     pl.semaphore_wait(barrier, signals)
 
@@ -209,10 +220,10 @@
 
     def take(slot, carry):
         out_u, out_d = carry
-        cell = cells_ref[slot]
+        cell = cells_ref[0, 0, slot]
         y = cell // cols
         x = cell - y * cols
-        alive = jnp.where(slot < count_ref[0], 1.0, 0.0).astype(f32)
+        alive = jnp.where(slot < count_ref[0, 0], 1.0, 0.0).astype(f32)
         px = jnp.full((1, 128), spacing * ((gx * cols + x).astype(f32) - (0.5 * cols * x_count - 0.5)), f32)
         py = jnp.full((1, 128), spacing * ((gy * rows + y).astype(f32) - (0.5 * rows * y_count - 0.5)), f32)
         radius = jnp.sqrt(px * px + py * py)
@@ -220,7 +231,8 @@
         weight_y = py / radius / (2.0 * spacing) * alive
         total_u = jnp.zeros((parts, 128), f32)
         total_d = jnp.zeros((parts, 128), f32)
-        for j in range(lane_blocks):
+        low = jnp.minimum(jnp.maximum(x - 1, 0) // 128, max(lane_blocks - 2, 0))
+        for j in [low + i for i in range(min(lane_blocks, 2))]:
             lane = iota((1, 128), 1) + 128 * j
             at = jnp.where(lane == x, alive, 0.0)
             along = jnp.where(lane == x + 1, weight_x, 0.0) - jnp.where(lane == x - 1, weight_x, 0.0)
@@ -235,7 +247,7 @@
         out_d = jnp.where(lane_p == slot, jnp.sum(total_d, axis=1, keepdims=True), out_d)
         return out_u, out_d
 
-    slots = cells_ref.shape[0]
+    slots = cells_ref.shape[2]
 
     half_kin = half_dt * kinetic
 
@@ -248,11 +260,11 @@
 
     def take_next(slot, carry):
         out_u, out_d = carry
-        cell = cells_ref[slot]
+        cell = cells_ref[0, 0, slot]
         row = cell // cols
         x = cell - row * cols
         y = jnp.maximum(row, 1)
-        alive = jnp.where(slot < count_ref[0], 1.0, 0.0).astype(f32)
+        alive = jnp.where(slot < count_ref[0, 0], 1.0, 0.0).astype(f32)
         px = jnp.full((1, 128), spacing * ((gx * cols + x).astype(f32) - (0.5 * cols * x_count - 0.5)), f32)
         py = jnp.full((1, 128), spacing * ((gy * rows + y).astype(f32) - (0.5 * rows * y_count - 0.5)), f32)
         radius = jnp.sqrt(px * px + py * py)
@@ -266,7 +278,8 @@
         plain = [zero, zero]
         scaled = [zero, zero]
         around = [zero, zero]
-        for j in range(lane_blocks):
+        low = jnp.minimum(jnp.maximum(x - 2, 0) // 128, max(lane_blocks - 2, 0))
+        for j in [low + i for i in range(min(lane_blocks, 2))]:
             lane = iota((1, 128), 1) + 128 * j
             at = jnp.where(lane == x, alive, 0.0)
             at_side = jnp.where((lane == x + 1) | (lane == x - 1), alive, 0.0)
@@ -320,7 +333,7 @@
         packed = jnp.where(lane8 < 64, turned[0:8], pltpu.roll(turned[8:16], 64, 1))
         if is_now:
             for slot in range(slots):
-                cell = cells_ref[slot]
+                cell = cells_ref[0, 0, slot]
                 y = cell // cols
                 x = cell - y * cols
                 px = spacing * ((gx * cols + x).astype(f32) - (0.5 * cols * x_count - 0.5))
@@ -329,7 +342,7 @@
                 row = sub8 == slot % 8
                 packed = jnp.where(row & (lane8 == base), px, packed)
                 packed = jnp.where(row & (lane8 == base + 1), py, packed)
-            packed = jnp.where(lane8 == 2 * parts + 2, count_ref[0].astype(f32), packed)
+            packed = jnp.where(lane8 == 2 * parts + 2, count_ref[0, 0].astype(f32), packed)
         target[column, gy, chip] = packed
 
     def chip_copy(buf, phase, k, source):
@@ -456,12 +469,21 @@
 
     def fix_columns(b, carry):
         rows_b = pl.ds(pl.multiple_of(b * 8 + top, 8), 8)
+        sides = []
         for p in range(parts):
+            other = (p + planes) % parts
             edge_w, edge_e = edges(0, p, b)
-            other = (p + planes) % parts
             scale = step_dt * kinetic if p < planes else -step_dt * kinetic
-            sec_v[0, other, rows_b, :] += jnp.where(first, scale * edge_w, 0.0)
-            sec_v[lane_blocks - 1, other, rows_b, :] += jnp.where(last, scale * edge_e, 0.0)
+            sides.append(
+                (
+                    other,
+                    sec_v[0, other, rows_b, :] + jnp.where(first, scale * edge_w, 0.0),
+                    sec_v[lane_blocks - 1, other, rows_b, :] + jnp.where(last, scale * edge_e, 0.0),
+                )
+            )
+        for other, low, high in sides:
+            sec_v[0, other, rows_b, :] = low
+            sec_v[lane_blocks - 1, other, rows_b, :] = high
         return carry
 
     surface(gather_0, True)
@@ -650,7 +672,8 @@
     me = lax.axis_index("gx") * y_count + lax.axis_index("gy")
     groups = count_ref.shape[0]
     slots = amp_ref.shape[0]
-    features = weight_ref.shape[1]
+    features = weight_ref.shape[1] // 8
+    feature = iota((128, 128), 1) < features
 
     def offset(i, at):
         return at + jnp.where(i < me, count_ref[i], 0)
@@ -663,30 +686,25 @@
         waves.append((plane.astype(f32) - 0.5 * (groups - 1)) * (k_span / groups))
 
     def gather_tile(t, n):
-        c = live_ref[0, t]
+        c = live_ref[0, t].astype(jnp.int32)
         at = pl.ds(pl.multiple_of(t * 8, 8), 8)
         block_0, block_1 = gather_0[at, :], gather_1[at, :]
-        to = pl.ds(pl.multiple_of(n * 8, 8), 8)
-        comp_0[to, :] = block_0
-        comp_1[to, :] = block_1
-        n = n + jnp.where(c > 0.5, 1, 0)
-        to = pl.ds(pl.multiple_of(n * 8, 8), 8)
-        comp_0[to, :] = pltpu.roll(block_0, 64, 1)
-        comp_1[to, :] = pltpu.roll(block_1, 64, 1)
-        return n + jnp.where(c > 8.5, 1, 0)
+        comp_0[pl.ds(n, 8), :] = block_0
+        comp_1[pl.ds(n, 8), :] = block_1
+        n = n + jnp.minimum(c, 8)
+        comp_0[pl.ds(n, 8), :] = pltpu.roll(block_0, 64, 1)
+        comp_1[pl.ds(n, 8), :] = pltpu.roll(block_1, 64, 1)
+        return n + jnp.maximum(c - 8, 0)
 
     live = lax.fori_loop(0, x_count * y_count, gather_tile, 0, unroll=8)
 
     def clear(i, carry):
-        to = pl.ds(pl.multiple_of((live + i) * 8, 8), 8)
+        to = pl.ds(live + i * 8, 8)
         comp_0[to, :] = jnp.zeros((8, 128), f32)
         comp_1[to, :] = jnp.zeros((8, 128), f32)
         return carry
 
     lax.fori_loop(0, 16, clear, 0)
-    for fetch, copy in copies:
-        fetch.wait()
-        copy.start()
     total[...] = jnp.zeros_like(total)
     kx = (iota((128, 128), 0).astype(f32) - 63.5) * (k_span / 128)
     sub8 = iota((8, 128), 0)
@@ -707,11 +725,16 @@
         right = []
         left = []
         for t, moment in enumerate((start_time, later_time)):
+            raw = jnp.where(feature, rows[t], 0.0)
+            high = raw.astype(jnp.bfloat16).astype(f32)
+            mid = (raw - high).astype(jnp.bfloat16).astype(f32)
+            low = (raw - high) - mid
+            side = (
+                (high + pltpu.roll(mid, features, 1))
+                + (pltpu.roll(low, 2 * features, 1) + pltpu.roll(high, 3 * features, 1))
+            ).astype(jnp.bfloat16)
             modes = jnp.dot(
-                rows[t][:, :features],
-                weight_ref[t],
-                precision=lax.Precision.HIGHEST,
-                preferred_element_type=f32,
+                jnp.concatenate([side, side], axis=1), weight_ref[t], preferred_element_type=f32
             )
             ur, ui, dr, di = (modes[:, 128 * i : 128 * i + 128] for i in range(4))
             right.append(
@@ -721,30 +744,38 @@
         right = jnp.concatenate(right, axis=0)
         rot_cos, rot_sin = turns(0.5 * ky * ky * moment8 - ky * py)
 
-        for s in range(slots):
-
-            @pl.when(s < own_count)
+        for first in range(0, slots, 2):
+
+            @pl.when(first < own_count)
             def _():
-                real = []
-                imag = []
-                for t in range(2):
-                    bc, bs = rot_cos[2 * s + t : 2 * s + t + 1], rot_sin[2 * s + t : 2 * s + t + 1]
-                    ac, as_ = left[t]
-                    real.append((ac * bc - as_ * bs).astype(jnp.bfloat16))
-                    imag.append((ac * bs + as_ * bc).astype(jnp.bfloat16))
-                q = jnp.concatenate(
-                    [jnp.concatenate(real, axis=1), jnp.concatenate(imag, axis=1)], axis=0
-                )
-                prod = jnp.dot(q, right, preferred_element_type=f32)
-                m = [prod[:128, 128 * i : 128 * i + 128] for i in range(6)]
-                w = [prod[128:, 128 * i : 128 * i + 128] for i in range(6)]
-                hy = waves[s]
-                total[s, 0] += kx * (m[0] - w[3]) + hy * (m[1] - w[4]) + (m[5] + w[2])
-                total[s, 1] += kx * (m[3] + w[0]) + hy * (m[4] + w[1]) - (m[2] - w[5])
+                sides = []
+                pair = range(first, min(first + 2, slots))
+                for s in pair:
+                    real = []
+                    imag = []
+                    for t in range(2):
+                        bc, bs = rot_cos[2 * s + t : 2 * s + t + 1], rot_sin[2 * s + t : 2 * s + t + 1]
+                        ac, as_ = left[t]
+                        real.append((ac * bc - as_ * bs).astype(jnp.bfloat16))
+                        imag.append((ac * bs + as_ * bc).astype(jnp.bfloat16))
+                    sides.append(jnp.concatenate(real, axis=1))
+                    sides.append(jnp.concatenate(imag, axis=1))
+                prod = jnp.dot(jnp.concatenate(sides, axis=0), right, preferred_element_type=f32)
+                for i, s in enumerate(pair):
+                    m = [prod[256 * i : 256 * i + 128, 128 * k : 128 * k + 128] for k in range(6)]
+                    w = [prod[256 * i + 128 : 256 * i + 256, 128 * k : 128 * k + 128] for k in range(6)]
+                    hy = waves[s]
+                    total[s, 0] += kx * (m[0] - w[3]) + hy * (m[1] - w[4]) + (m[5] + w[2])
+                    total[s, 1] += kx * (m[3] + w[0]) + hy * (m[4] + w[1]) - (m[2] - w[5])
 
         return carry
 
-    lax.fori_loop(0, (live + 15) // 16, chunk, 0)
+    chunks = (live + 127) // 128
+    lax.fori_loop(0, jnp.minimum(chunks, 1), chunk, 0)
+    for fetch, copy in copies:
+        fetch.wait()
+        copy.start()
+    lax.fori_loop(1, chunks, chunk, 0)
     for s in range(slots):
         for part in range(2):
             sl = pl.ds(part, 128, stride=2)
@@ -801,8 +832,8 @@
         ),
         name="step",
     )(
-        surf_cells.reshape(slots),
-        surf_count.reshape(1),
+        surf_cells,
+        surf_count,
         psi_now.reshape(parts, rows, cols),
         potential,
     )

time: 44.9 us -> 41.5 us (0.924)
  the two profiles are of different devices: /device:TPU:32 before, /device:TPU:1 now
where the time goes in v3:
time: 41.5 us; the launch traced here: 41.3 us
  Pallas kernels  39.2 us (94%)
  between operations  1.39 us (3%)
  local copies, waits for them, and re-layouts  0.66 us (2%)
    pallas_call x1, Pallas kernels, shards(): pl.pallas_call(functools.partial(step_kernel, x_count, y_count), out_shap...  32.5 us
    pallas_call x1, Pallas kernels, shards(): pl.pallas_call(functools.partial(flux_kernel, x_count, y_count), out_shap...  6.76 us

profile of v3, /device:TPU:1, one launch (start us, length us, event | category | flops | bytes accessed | tf_op | source)
XLA Modules:
  0.0 41.3 jit_solution(9450440002834536454)
XLA Ops:
  0.6 0.0 copy-start
  0.6 0.0 copy-start.2
  0.7 0.0 copy-start.1
  1.4 0.0 copy-start.3
  1.4 0.6 %copy-done.3 = s32[1,1,16]{2,1,0:T(1,128)S(1)} copy-done((s32[1,1,16]{2,1,0:T(1,128)S(1)}, s32[1,1,16]{2,1,0:T(1,128)}, u32[]{:S(2)}) %copy-start.3) | copy-done | bytes 88
  2.0 32.5 %step.1 = (f32[16,192,384]{2,1,0:T(8,128)}, f32[2,16,4,8,128]{4,3,2,1,0:T(8,128)S(1)}, f32[2,16,4,8,128]{4,3,2,1,0:T(8,128)S(1)}, f32[8,128]{1,0:T(8,128)S(1)}) custom-call(s32[1,1,16]{2,1,0:T(1,128)S(1)} %copy-done.3, s32[1,1]{1,0:T(1,128)S(6)} %copy.10.count_ref, f32[16,192,384]{2,1,0:T(8,128)} %bitcast.8, f32[8,192,384]{2,1,0:T(8,128)} %pot_hbm.1), custom_call_target="tpu_custom_call" | custom-call | tf_op jit(solution)/shard_map/step/pallas_call | solution.py:802
  34.5 0.0 copy-done
  34.5 0.0 copy-done.2
  34.5 0.0 copy-done.1
  34.5 6.8 %flux.1 = (f32[16,192,384]{2,1,0:T(8,128)}, f32[4,256,128]{2,1,0:T(8,128)}) custom-call(f32[8,128]{1,0:T(8,128)S(1)} %get-tuple-element.8.live_ref, s32[128]{0:T(128)S(1)} %copy-done.1, s32[128]{0:T(128)S(1)} %copy-done.2, f32[1024,128]{1,0:T(8,128)S(1)} %bitcast.6, f32[1024,128]{1,0:T(8,128)S(1)} %bitcast.7, bf16[2,256,512]{2,1,0:T(8,128)(2,1)S(1)} %copy-done, ...), custom_call_target="tpu_custom_call" | custom-call | tf_op jit(solution)/shard_map/flux/pallas_call | solution.py:841
Async XLA Ops:
  0.6 33.9 %copy-start = (bf16[2,256,512]{2,1,0:T(8,128)(2,1)S(1)}, bf16[2,256,512]{2,1,0:T(8,128)(2,1)}, u32[]{:S(2)}) copy-start(bf16[2,256,512]{2,1,0:T(8,128)(2,1)} %constant.2.clone.weight_ref) | copy-start | bytes 1572868
  0.6 33.9 %copy-start.2 = (s32[128]{0:T(128)S(1)}, s32[128]{0:T(128)}, u32[]{:S(2)}) copy-start(s32[128]{0:T(128)} %order_ref.1) | copy-start | bytes 1540
  0.7 33.9 %copy-start.1 = (s32[128]{0:T(128)S(1)}, s32[128]{0:T(128)}, u32[]{:S(2)}) copy-start(s32[128]{0:T(128)} %count_ref.2) | copy-start | bytes 1540
  1.4 0.7 %copy-start.3 = (s32[1,1,16]{2,1,0:T(1,128)S(1)}, s32[1,1,16]{2,1,0:T(1,128)}, u32[]{:S(2)}) copy-start(s32[1,1,16]{2,1,0:T(1,128)} %cells_ref.1) | copy-start | bytes 196

commit v4 on v3

--- a/solution.py
+++ b/solution.py
@@ -102,7 +102,8 @@
     west, east = wrap(gx - 1, x_count), wrap(gx + 1, x_count)
     north, south = wrap(gy - 1, y_count), wrap(gy + 1, y_count)
     loads = []
-    for j in range(lane_blocks):
+    load_order = [0, lane_blocks - 1] + list(range(1, lane_blocks - 1))
+    for j in load_order:
         sl = slice(128 * j, 128 * j + 128)
         loads.append(
             pltpu.make_async_copy(
@@ -119,32 +120,19 @@
     chip = gx // 2
     chips = x_count // 2
     signals = 0
-    for k in range(1, chips):
-        pl.semaphore_signal(
-            barrier, inc=1, device_id=(wrap(gx + 2 * k, x_count), gy), device_id_type=MESH
-        )
+    for k in range(1, x_count):
+        pl.semaphore_signal(barrier, inc=1, device_id=(wrap(gx + k, x_count), gy), device_id_type=MESH)
         signals += 1
     for k in range(1, y_count):
         pl.semaphore_signal(barrier, inc=1, device_id=(gx, wrap(gy + k, y_count)), device_id_type=MESH)
         signals += 1
     for sx in (west, east):
-        for sy in (north, gy, south):
+        for sy in (north, south):
             pl.semaphore_signal(barrier, inc=1, device_id=(sx, sy), device_id_type=MESH)
             signals += 1
 
-    for copy in loads:
+    for copy in loads[:4]:
         copy.wait()
-
-    for side, (near, far) in enumerate(((top, top + 1), (top + rows - 1, top + rows - 2))):
-        for j in range(lane_blocks):
-            sl = slice(128 * j, 128 * j + 128)
-            for p in range(parts):
-                row_msg[side, p : p + 1, sl] = psi_v[j, p, near : near + 1, :]
-                row_msg[side, parts + p : parts + p + 1, sl] = psi_v[j, p, far : far + 1, :]
-            for z in range(planes):
-                row_msg[side, 2 * parts + z : 2 * parts + z + 1, sl] = pot_v[
-                    j, z, near - top : near - top + 1, :
-                ]
 
     lane8 = iota((8, 128), 1)
     sub8 = iota((8, 128), 0)
@@ -178,6 +166,32 @@
     pl.semaphore_wait(barrier, signals)
 
     halo = []
+    for side, target in enumerate((west, east)):
+        halo.append(
+            pltpu.make_async_remote_copy(
+                src_ref=col_msg.at[side],
+                dst_ref=col_got.at[1 - side],
+                send_sem=col_send.at[side],
+                recv_sem=col_recv.at[1 - side],
+                device_id=(target, gy),
+                device_id_type=MESH,
+            )
+        )
+    for copy in halo:
+        copy.start()
+    for copy in loads[4:]:
+        copy.wait()
+    for side, (near, far) in enumerate(((top, top + 1), (top + rows - 1, top + rows - 2))):
+        for j in range(lane_blocks):
+            sl = slice(128 * j, 128 * j + 128)
+            for p in range(parts):
+                row_msg[side, p : p + 1, sl] = psi_v[j, p, near : near + 1, :]
+                row_msg[side, parts + p : parts + p + 1, sl] = psi_v[j, p, far : far + 1, :]
+            for z in range(planes):
+                row_msg[side, 2 * parts + z : 2 * parts + z + 1, sl] = pot_v[
+                    j, z, near - top : near - top + 1, :
+                ]
+
     for side, target in enumerate((north, south)):
         halo.append(
             pltpu.make_async_remote_copy(
@@ -186,17 +200,6 @@
                 send_sem=row_send.at[side],
                 recv_sem=row_recv.at[1 - side],
                 device_id=(gx, target),
-                device_id_type=MESH,
-            )
-        )
-    for side, target in enumerate((west, east)):
-        halo.append(
-            pltpu.make_async_remote_copy(
-                src_ref=col_msg.at[side],
-                dst_ref=col_got.at[1 - side],
-                send_sem=col_send.at[side],
-                recv_sem=col_recv.at[1 - side],
-                device_id=(target, gy),
                 device_id_type=MESH,
             )
         )
@@ -213,7 +216,7 @@
                     device_id_type=MESH,
                 )
             )
-    for copy in halo:
+    for copy in halo[2:]:
         copy.start()
 
     lane_p = iota((parts, 128), 1)
@@ -325,13 +328,17 @@
     def surface(target, is_now):
         zero = jnp.zeros((parts, 128), f32)
         out_u, out_d = lax.fori_loop(
-            0, slots, take if is_now else take_next, (zero, zero), unroll=4 if is_now else 2
+            0, slots, take if is_now else take_next, (zero, zero), unroll=8
         )
         turned = jnp.transpose(
             jnp.concatenate([out_u, out_d, jnp.zeros((128 - 2 * parts, 128), f32)], axis=0)
         )
-        packed = jnp.where(lane8 < 64, turned[0:8], pltpu.roll(turned[8:16], 64, 1))
+        if not is_now:
+            target[gy, gx] = (turned[0:4] + pltpu.roll(turned[4:8], 32, 1)) + (
+                pltpu.roll(turned[8:12], 64, 1) + pltpu.roll(turned[12:16], 96, 1)
+            )
         if is_now:
+            packed = jnp.where(lane8 < 64, turned[0:8], pltpu.roll(turned[8:16], 64, 1))
             for slot in range(slots):
                 cell = cells_ref[0, 0, slot]
                 y = cell // cols
@@ -343,7 +350,7 @@
                 packed = jnp.where(row & (lane8 == base), px, packed)
                 packed = jnp.where(row & (lane8 == base + 1), py, packed)
             packed = jnp.where(lane8 == 2 * parts + 2, count_ref[0, 0].astype(f32), packed)
-        target[column, gy, chip] = packed
+            target[column, gy, chip] = packed
 
     def chip_copy(buf, phase, k, source):
         return pltpu.make_async_remote_copy(
@@ -392,6 +399,26 @@
 
     def hop_end(buf, phase):
         pair_copy(buf, phase, 1 - column).wait_recv()
+
+    def line_copy(k, source):
+        return pltpu.make_async_remote_copy(
+            src_ref=gather_1.at[gy, source],
+            dst_ref=gather_1.at[gy, source],
+            send_sem=x_send.at[1, k],
+            recv_sem=x_recv.at[1, k],
+            device_id=(wrap(gx + k, x_count), gy),
+            device_id_type=MESH,
+        )
+
+    def sheet_copy(k, source):
+        return pltpu.make_async_remote_copy(
+            src_ref=gather_1.at[source],
+            dst_ref=gather_1.at[source],
+            send_sem=y_send.at[1, k],
+            recv_sem=y_recv.at[1, k],
+            device_id=(gx, wrap(gy + k, y_count)),
+            device_id_type=MESH,
+        )
 
     def sends_wait(buf, phase):
         for k in range(1, chips):
@@ -581,7 +608,8 @@
 
     lax.fori_loop(0, blocks, fix_columns, 0, unroll=2)
     surface(gather_1, False)
-    hop_1(gather_1, 1)
+    for k in range(1, x_count):
+        line_copy(k, gx).start()
     stores = []
     pieces = 4
     per = blocks // pieces
@@ -597,7 +625,10 @@
             )
             stores[-1].start()
         if q == 0:
-            hop_2(gather_1, 1)
+            for k in range(1, x_count):
+                line_copy(k, wrap(gx - k, x_count)).wait_recv()
+            for k in range(1, y_count):
+                sheet_copy(k, gy).start()
             hop_3(gather_0, 0)
     hop_end(gather_0, 0)
 
@@ -608,14 +639,17 @@
         return total
 
     live_ref[...] = lax.fori_loop(0, y_count, count_row, jnp.zeros((8, 128), f32))
-    hop_3(gather_1, 1)
     for copy in halo:
         copy.wait_send()
     for copy in stores:
         copy.wait()
-    hop_end(gather_1, 1)
+    for k in range(1, y_count):
+        sheet_copy(k, wrap(gy - k, y_count)).wait_recv()
     sends_wait(gather_0, 0)
-    sends_wait(gather_1, 1)
+    for k in range(1, x_count):
+        line_copy(k, gx).wait_send()
+    for k in range(1, y_count):
+        sheet_copy(k, gy).wait_send()
 
 
 def turns(phase):
@@ -685,15 +719,22 @@
         plane = order_ref[jnp.minimum(own_start + s, groups - 1)]
         waves.append((plane.astype(f32) - 0.5 * (groups - 1)) * (k_span / groups))
 
+    tiles = x_count * y_count
+    chips = x_count // 2
+
     def gather_tile(t, n):
         c = live_ref[0, t].astype(jnp.int32)
         at = pl.ds(pl.multiple_of(t * 8, 8), 8)
-        block_0, block_1 = gather_0[at, :], gather_1[at, :]
+        block_0 = gather_0[at, :]
+        half, row, chip = t // (tiles // 2), (t // chips) % y_count, t % chips
+        block_1 = gather_1[row * x_count + 2 * chip + half]
         comp_0[pl.ds(n, 8), :] = block_0
-        comp_1[pl.ds(n, 8), :] = block_1
+        comp_1[pl.ds(n, 4), :] = block_1
+        comp_1[pl.ds(n + 4, 4), :] = pltpu.roll(block_1, 96, 1)
         n = n + jnp.minimum(c, 8)
         comp_0[pl.ds(n, 8), :] = pltpu.roll(block_0, 64, 1)
-        comp_1[pl.ds(n, 8), :] = pltpu.roll(block_1, 64, 1)
+        comp_1[pl.ds(n, 4), :] = pltpu.roll(block_1, 64, 1)
+        comp_1[pl.ds(n + 4, 4), :] = pltpu.roll(block_1, 32, 1)
         return n + jnp.maximum(c - 8, 0)
 
     live = lax.fori_loop(0, x_count * y_count, gather_tile, 0, unroll=8)
@@ -798,10 +839,11 @@
     hbm = pl.BlockSpec(memory_space=pltpu.HBM)
     dma = pltpu.SemaphoreType.DMA
     gathered = jax.ShapeDtypeStruct((2, y_count, x_count // 2, 8, 128), f32)
+    sheet = jax.ShapeDtypeStruct((y_count, x_count, 4, 128), f32)
     field = jax.ShapeDtypeStruct((parts, rows, cols), f32)
     staged, gather_0, gather_1, live = pl.pallas_call(
         functools.partial(step_kernel, x_count, y_count),
-        out_shape=(field, gathered, gathered, jax.ShapeDtypeStruct((8, 128), f32)),
+        out_shape=(field, gathered, sheet, jax.ShapeDtypeStruct((8, 128), f32)),
         in_specs=[smem, smem, hbm, hbm],
         out_specs=(any_spec, vmem, vmem, vmem),
         scratch_shapes=[
@@ -858,7 +900,7 @@
         block_count,
         block_order,
         gather_0.reshape(tiles * 8, 128),
-        gather_1.reshape(tiles * 8, 128),
+        gather_1.reshape(tiles, 4, 128),
         jnp.asarray(mode_weights(planes, modes_z)),
         amplitude.reshape(own, 2 * modes_x, modes_z),
         staged,

time: 41.5 us -> 39.3 us (0.947); the launches traced: 41.3 us -> 38.6 us
  Pallas kernels: 39.2 us -> 36.5 us
    pallas_call x1, Pallas kernels: 32.5 us -> 29.4 us  [shards(): pl.pallas_call(functools.partial(step_kernel, x_count, y_count), out_shap...]
where the time goes in v4:
time: 39.3 us; the launch traced here: 38.6 us
  Pallas kernels  36.5 us (93%)
  between operations  1.44 us (4%)
  local copies, waits for them, and re-layouts  0.67 us (2%)
    pallas_call x1, Pallas kernels, shards(): pl.pallas_call(functools.partial(step_kernel, x_count, y_count), out_shap...  29.4 us
    pallas_call x1, Pallas kernels, shards(): pl.pallas_call(functools.partial(flux_kernel, x_count, y_count), out_shap...  7.1 us

profile of v4, /device:TPU:1, one launch (start us, length us, event | category | flops | bytes accessed | tf_op | source)
XLA Modules:
  0.0 38.6 jit_solution(15101856237705188799)
XLA Ops:
  0.6 0.0 copy-start.1
  0.6 0.0 copy-start
  0.7 0.0 copy-start.3
  0.7 0.0 copy-start.2
  1.4 0.0 copy-start.4
  1.4 0.6 %copy-done.4 = s32[1,1,16]{2,1,0:T(1,128)S(1)} copy-done((s32[1,1,16]{2,1,0:T(1,128)S(1)}, s32[1,1,16]{2,1,0:T(1,128)}, u32[]{:S(2)}) %copy-start.4) | copy-done | bytes 88
  2.1 29.4 %step.1 = (f32[16,192,384]{2,1,0:T(8,128)}, f32[2,16,4,8,128]{4,3,2,1,0:T(8,128)S(1)}, f32[16,8,4,128]{3,2,1,0:T(4,128)S(1)}, f32[8,128]{1,0:T(8,128)S(1)}) custom-call(s32[1,1,16]{2,1,0:T(1,128)S(1)} %copy-done.4, s32[1,1]{1,0:T(1,128)S(6)} %copy.10.count_ref, f32[16,192,384]{2,1,0:T(8,128)} %bitcast.9, f32[8,192,384]{2,1,0:T(8,128)} %pot_hbm.1), custom_call_target="tpu_custom_call" | custom-call | tf_op jit(solution)/shard_map/step/pallas_call | solution.py:844
  31.4 0.0 copy-done.1
  31.4 0.0 copy-done
  31.5 0.0 copy-done.3
  31.5 0.0 copy-done.2
  31.5 7.1 %flux.1 = (f32[16,192,384]{2,1,0:T(8,128)}, f32[4,256,128]{2,1,0:T(8,128)}) custom-call(f32[8,128]{1,0:T(8,128)S(1)} %get-tuple-element.8.live_ref, s32[128]{0:T(128)S(1)} %copy-done.2, s32[128]{0:T(128)S(1)} %copy-done.3, f32[1024,128]{1,0:T(8,128)S(1)} %bitcast.7, f32[128,4,128]{2,1,0:T(4,128)S(1)} %bitcast.8, bf16[2,256,512]{2,1,0:T(8,128)(2,1)S(1)} %copy-done.1, ...), custom_call_target="tpu_custom_call" | custom-call | tf_op jit(solution)/shard_map/flux/pallas_call | solution.py:883
Async XLA Ops:
  0.6 30.8 %copy-start.1 = (bf16[2,256,512]{2,1,0:T(8,128)(2,1)S(1)}, bf16[2,256,512]{2,1,0:T(8,128)(2,1)}, u32[]{:S(2)}) copy-start(bf16[2,256,512]{2,1,0:T(8,128)(2,1)} %constant.2.clone.weight_ref) | copy-start | bytes 1572868
  0.6 30.8 %copy-start = (f32[4,128,2,128]{3,2,1,0:T(2,128)S(1)}, f32[4,128,2,128]{3,2,1,0:T(2,128)}, u32[]{:S(2)}) copy-start(f32[4,128,2,128]{3,2,1,0:T(2,128)} %param.14) | copy-start | bytes 1572868
  0.7 30.8 %copy-start.3 = (s32[128]{0:T(128)S(1)}, s32[128]{0:T(128)}, u32[]{:S(2)}) copy-start(s32[128]{0:T(128)} %order_ref.1) | copy-start | bytes 1540
  0.7 30.8 %copy-start.2 = (s32[128]{0:T(128)S(1)}, s32[128]{0:T(128)}, u32[]{:S(2)}) copy-start(s32[128]{0:T(128)} %count_ref.2) | copy-start | bytes 1540
  1.4 0.7 %copy-start.4 = (s32[1,1,16]{2,1,0:T(1,128)S(1)}, s32[1,1,16]{2,1,0:T(1,128)}, u32[]{:S(2)}) copy-start(s32[1,1,16]{2,1,0:T(1,128)} %cells_ref.1) | copy-start | bytes 196

commit v5 on v4

--- a/solution.py
+++ b/solution.py
@@ -102,15 +102,21 @@
     west, east = wrap(gx - 1, x_count), wrap(gx + 1, x_count)
     north, south = wrap(gy - 1, y_count), wrap(gy + 1, y_count)
     loads = []
-    load_order = [0, lane_blocks - 1] + list(range(1, lane_blocks - 1))
-    for j in load_order:
+    halves = 2
+    part_rows = rows // halves
+    load_parts = [(j, h) for h in range(halves) for j in (0, lane_blocks - 1)]
+    load_parts += [(j, h) for j in range(1, lane_blocks - 1) for h in range(halves)]
+    for j, h in load_parts:
         sl = slice(128 * j, 128 * j + 128)
+        lo, hi = h * part_rows, (h + 1) * part_rows
         loads.append(
             pltpu.make_async_copy(
-                psi_hbm.at[:, :, sl], psi_v.at[j, :, top : top + rows, :], load_sem.at[0, j]
-            )
-        )
-        loads.append(pltpu.make_async_copy(pot_hbm.at[:, :, sl], pot_v.at[j], load_sem.at[1, j]))
+                psi_hbm.at[:, lo:hi, sl], psi_v.at[j, :, top + lo : top + hi, :], load_sem.at[0, h, j]
+            )
+        )
+        loads.append(
+            pltpu.make_async_copy(pot_hbm.at[:, lo:hi, sl], pot_v.at[j, :, lo:hi, :], load_sem.at[1, h, j])
+        )
     for copy in loads:
         copy.start()
 
@@ -131,8 +137,6 @@
             pl.semaphore_signal(barrier, inc=1, device_id=(sx, sy), device_id_type=MESH)
             signals += 1
 
-    for copy in loads[:4]:
-        copy.wait()
 
     lane8 = iota((8, 128), 1)
     sub8 = iota((8, 128), 0)
@@ -161,7 +165,10 @@
             col_msg[side, pl.ds(r0, 8), :] = packed
         return carry
 
-    lax.fori_loop(0, blocks, pack, 0, unroll=4)
+    for h in range(halves):
+        for copy in loads[4 * h : 4 * h + 4]:
+            copy.wait()
+        lax.fori_loop(h * (blocks // halves), (h + 1) * (blocks // halves), pack, 0, unroll=4)
 
     pl.semaphore_wait(barrier, signals)
 
@@ -179,7 +186,7 @@
         )
     for copy in halo:
         copy.start()
-    for copy in loads[4:]:
+    for copy in loads[4 * halves :]:
         copy.wait()
     for side, (near, far) in enumerate(((top, top + 1), (top + rows - 1, top + rows - 2))):
         for j in range(lane_blocks):
@@ -606,7 +613,7 @@
             )
         ) * keep
 
-    lax.fori_loop(0, blocks, fix_columns, 0, unroll=2)
+    lax.fori_loop(0, blocks, fix_columns, 0, unroll=4)
     surface(gather_1, False)
     for k in range(1, x_count):
         line_copy(k, gx).start()
@@ -712,7 +719,7 @@
     def offset(i, at):
         return at + jnp.where(i < me, count_ref[i], 0)
 
-    own_start = lax.fori_loop(0, groups, offset, 0, unroll=8)
+    own_start = lax.fori_loop(0, groups, offset, 0, unroll=True)
     own_count = count_ref[me]
     waves = []
     for s in range(slots):
@@ -737,7 +744,7 @@
         comp_1[pl.ds(n + 4, 4), :] = pltpu.roll(block_1, 32, 1)
         return n + jnp.maximum(c - 8, 0)
 
-    live = lax.fori_loop(0, x_count * y_count, gather_tile, 0, unroll=8)
+    live = lax.fori_loop(0, x_count * y_count, gather_tile, 0, unroll=True)
 
     def clear(i, carry):
         to = pl.ds(live + i * 8, 8)
@@ -856,7 +863,7 @@
             pltpu.VMEM((2, rows, 128), f32),
             pltpu.VMEM((4, parts, 128), f32),
             pltpu.VMEM((2, 2, rows, 128), f32),
-            dma((2, cols // 128)),
+            dma((2, 2, cols // 128)),
             dma((4, cols // 128)),
             dma((2,)),
             dma((2,)),

time: 39.3 us -> 38 us (0.967); the launches traced: 38.6 us -> 37.9 us
  Pallas kernels: 36.5 us -> 35.8 us
    pallas_call x1, Pallas kernels: 29.4 us -> 28.4 us  [shards(): pl.pallas_call(functools.partial(step_kernel, x_count, y_count), out_shap...]
where the time goes in v5:
time: 38 us; the launch traced here: 37.9 us
  Pallas kernels  35.8 us (94%)
  between operations  1.44 us (4%)
  local copies, waits for them, and re-layouts  0.67 us (2%)
    pallas_call x1, Pallas kernels, shards(): pl.pallas_call(functools.partial(step_kernel, x_count, y_count), out_shap...  28.4 us
    pallas_call x1, Pallas kernels, shards(): pl.pallas_call(functools.partial(flux_kernel, x_count, y_count), out_shap...  7.34 us

profile of v5, /device:TPU:1, one launch (start us, length us, event | category | flops | bytes accessed | tf_op | source)
XLA Modules:
  0.0 37.9 jit_solution(4241991678380055523)
XLA Ops:
  0.6 0.0 copy-start.1
  0.6 0.0 copy-start
  0.7 0.0 copy-start.3
  0.7 0.0 copy-start.2
  1.4 0.0 copy-start.4
  1.4 0.6 %copy-done.4 = s32[1,1,16]{2,1,0:T(1,128)S(1)} copy-done((s32[1,1,16]{2,1,0:T(1,128)S(1)}, s32[1,1,16]{2,1,0:T(1,128)}, u32[]{:S(2)}) %copy-start.4) | copy-done | bytes 88
  2.1 28.4 %step.1 = (f32[16,192,384]{2,1,0:T(8,128)}, f32[2,16,4,8,128]{4,3,2,1,0:T(8,128)S(1)}, f32[16,8,4,128]{3,2,1,0:T(4,128)S(1)}, f32[8,128]{1,0:T(8,128)S(1)}) custom-call(s32[1,1,16]{2,1,0:T(1,128)S(1)} %copy-done.4, s32[1,1]{1,0:T(1,128)S(6)} %copy.10.count_ref, f32[16,192,384]{2,1,0:T(8,128)} %bitcast.9, f32[8,192,384]{2,1,0:T(8,128)} %pot_hbm.1), custom_call_target="tpu_custom_call" | custom-call | tf_op jit(solution)/shard_map/step/pallas_call | solution.py:851
  30.5 0.0 copy-done.1
  30.5 0.0 copy-done
  30.5 0.0 copy-done.3
  30.5 0.0 copy-done.2
  30.6 7.3 %flux.1 = (f32[16,192,384]{2,1,0:T(8,128)}, f32[4,256,128]{2,1,0:T(8,128)}) custom-call(f32[8,128]{1,0:T(8,128)S(1)} %get-tuple-element.8.live_ref, s32[128]{0:T(128)S(1)} %copy-done.2, s32[128]{0:T(128)S(1)} %copy-done.3, f32[1024,128]{1,0:T(8,128)S(1)} %bitcast.7, f32[128,4,128]{2,1,0:T(4,128)S(1)} %bitcast.8, bf16[2,256,512]{2,1,0:T(8,128)(2,1)S(1)} %copy-done.1, ...), custom_call_target="tpu_custom_call" | custom-call | tf_op jit(solution)/shard_map/flux/pallas_call | solution.py:890
Async XLA Ops:
  0.6 29.9 %copy-start.1 = (bf16[2,256,512]{2,1,0:T(8,128)(2,1)S(1)}, bf16[2,256,512]{2,1,0:T(8,128)(2,1)}, u32[]{:S(2)}) copy-start(bf16[2,256,512]{2,1,0:T(8,128)(2,1)} %constant.2.clone.weight_ref) | copy-start | bytes 1572868
  0.6 29.9 %copy-start = (f32[4,128,2,128]{3,2,1,0:T(2,128)S(1)}, f32[4,128,2,128]{3,2,1,0:T(2,128)}, u32[]{:S(2)}) copy-start(f32[4,128,2,128]{3,2,1,0:T(2,128)} %param.14) | copy-start | bytes 1572868
  0.7 29.9 %copy-start.3 = (s32[128]{0:T(128)S(1)}, s32[128]{0:T(128)}, u32[]{:S(2)}) copy-start(s32[128]{0:T(128)} %order_ref.1) | copy-start | bytes 1540
  0.7 29.9 %copy-start.2 = (s32[128]{0:T(128)S(1)}, s32[128]{0:T(128)}, u32[]{:S(2)}) copy-start(s32[128]{0:T(128)} %count_ref.2) | copy-start | bytes 1540
  1.4 0.7 %copy-start.4 = (s32[1,1,16]{2,1,0:T(1,128)S(1)}, s32[1,1,16]{2,1,0:T(1,128)}, u32[]{:S(2)}) copy-start(s32[1,1,16]{2,1,0:T(1,128)} %cells_ref.1) | copy-start | bytes 196

commit v6 on v5

--- a/solution.py
+++ b/solution.py
@@ -335,7 +335,7 @@
     def surface(target, is_now):
         zero = jnp.zeros((parts, 128), f32)
         out_u, out_d = lax.fori_loop(
-            0, slots, take if is_now else take_next, (zero, zero), unroll=8
+            0, slots, take if is_now else take_next, (zero, zero), unroll=True
         )
         turned = jnp.transpose(
             jnp.concatenate([out_u, out_d, jnp.zeros((128 - 2 * parts, 128), f32)], axis=0)

time: 38 us -> 37.7 us (level)
  Pallas kernels: 35.8 us -> 35.3 us
    pallas_call x1, Pallas kernels: 7.34 us -> 6.91 us  [shards(): pl.pallas_call(functools.partial(flux_kernel, x_count, y_count), out_shap...]
where the time goes in v6:
time: 37.7 us; the launch traced here: 37.4 us
  Pallas kernels  35.3 us (94%)
  between operations  1.44 us (4%)
  local copies, waits for them, and re-layouts  0.67 us (2%)
    pallas_call x1, Pallas kernels, shards(): pl.pallas_call(functools.partial(step_kernel, x_count, y_count), out_shap...  28.4 us
    pallas_call x1, Pallas kernels, shards(): pl.pallas_call(functools.partial(flux_kernel, x_count, y_count), out_shap...  6.91 us

profile of v6, /device:TPU:1, one launch (start us, length us, event | category | flops | bytes accessed | tf_op | source)
XLA Modules:
  0.0 37.4 jit_solution(13987105941181022620)
XLA Ops:
  0.6 0.0 copy-start.1
  0.6 0.0 copy-start
  0.7 0.0 copy-start.3
  0.7 0.0 copy-start.2
  1.4 0.0 copy-start.4
  1.4 0.6 %copy-done.4 = s32[1,1,16]{2,1,0:T(1,128)S(1)} copy-done((s32[1,1,16]{2,1,0:T(1,128)S(1)}, s32[1,1,16]{2,1,0:T(1,128)}, u32[]{:S(2)}) %copy-start.4) | copy-done | bytes 88
  2.1 28.4 %step.1 = (f32[16,192,384]{2,1,0:T(8,128)}, f32[2,16,4,8,128]{4,3,2,1,0:T(8,128)S(1)}, f32[16,8,4,128]{3,2,1,0:T(4,128)S(1)}, f32[8,128]{1,0:T(8,128)S(1)}) custom-call(s32[1,1,16]{2,1,0:T(1,128)S(1)} %copy-done.4, s32[1,1]{1,0:T(1,128)S(6)} %copy.10.count_ref, f32[16,192,384]{2,1,0:T(8,128)} %bitcast.9, f32[8,192,384]{2,1,0:T(8,128)} %pot_hbm.1), custom_call_target="tpu_custom_call" | custom-call | tf_op jit(solution)/shard_map/step/pallas_call | solution.py:851
  30.5 0.0 copy-done.1
  30.5 0.0 copy-done
  30.5 0.0 copy-done.3
  30.5 0.0 copy-done.2
  30.5 6.9 %flux.1 = (f32[16,192,384]{2,1,0:T(8,128)}, f32[4,256,128]{2,1,0:T(8,128)}) custom-call(f32[8,128]{1,0:T(8,128)S(1)} %get-tuple-element.8.live_ref, s32[128]{0:T(128)S(1)} %copy-done.2, s32[128]{0:T(128)S(1)} %copy-done.3, f32[1024,128]{1,0:T(8,128)S(1)} %bitcast.7, f32[128,4,128]{2,1,0:T(4,128)S(1)} %bitcast.8, bf16[2,256,512]{2,1,0:T(8,128)(2,1)S(1)} %copy-done.1, ...), custom_call_target="tpu_custom_call" | custom-call | tf_op jit(solution)/shard_map/flux/pallas_call | solution.py:890
Async XLA Ops:
  0.6 29.8 %copy-start.1 = (bf16[2,256,512]{2,1,0:T(8,128)(2,1)S(1)}, bf16[2,256,512]{2,1,0:T(8,128)(2,1)}, u32[]{:S(2)}) copy-start(bf16[2,256,512]{2,1,0:T(8,128)(2,1)} %constant.2.clone.weight_ref) | copy-start | bytes 1572868
  0.6 29.8 %copy-start = (f32[4,128,2,128]{3,2,1,0:T(2,128)S(1)}, f32[4,128,2,128]{3,2,1,0:T(2,128)}, u32[]{:S(2)}) copy-start(f32[4,128,2,128]{3,2,1,0:T(2,128)} %param.14) | copy-start | bytes 1572868
  0.7 29.8 %copy-start.3 = (s32[128]{0:T(128)S(1)}, s32[128]{0:T(128)}, u32[]{:S(2)}) copy-start(s32[128]{0:T(128)} %order_ref.1) | copy-start | bytes 1540
  0.7 29.8 %copy-start.2 = (s32[128]{0:T(128)S(1)}, s32[128]{0:T(128)}, u32[]{:S(2)}) copy-start(s32[128]{0:T(128)} %count_ref.2) | copy-start | bytes 1540
  1.4 0.7 %copy-start.4 = (s32[1,1,16]{2,1,0:T(1,128)S(1)}, s32[1,1,16]{2,1,0:T(1,128)}, u32[]{:S(2)}) copy-start(s32[1,1,16]{2,1,0:T(1,128)} %cells_ref.1) | copy-start | bytes 196
